TPU v7x, 256 devices: a whole 4x4x8 slice. The times are simulated.
256 devices in a mesh: lon: 16 (over y_hi, z), lev: 4 (over x), lat: 4 (over y_lo, core).
Axes of the slice: x: 4, y: 4 (y_hi: 2, y_lo: 2; y = y_hi * 2 + y_lo), z: 8, core: 2. Of those that a mesh axis runs over, the one named last changes fastest.
Arguments:
- tokens: bfloat16 [2, 8, 48, 192, 192], P(None, 'lev', 'lat', 'lon'), may hold values from -40 to 40
- cotangent: bfloat16 [2, 8, 48, 192, 192], P(None, 'lev', 'lat', 'lon'), may hold values from -6 to 6
- w_qkv: bfloat16 [192, 576], replicated, may hold values from -0.4375 to 0.4375
- w_proj: bfloat16 [192, 192], replicated, may hold values from -0.4375 to 0.4375
- ln_gain: float32 [192], replicated, may hold values from 0.1 to 1.9
- ln_shift: float32 [192], replicated, may hold values from -3 to 3
- bias_table: float32 [32, 6, 3312], P(('lev', 'lat')), may hold values from -4 to 302
- region_ids: int32 [8, 48], P('lev', 'lat'), may hold values from 0 to 3
- lat_keep: int32 [48], P('lat'), may hold values 0 or 1
Outputs:
- grad_tokens: bfloat16 [2, 8, 48, 192, 192], P(None, 'lev', 'lat', 'lon')
- grad_qkv: float32 [192, 576], replicated
- grad_proj: float32 [192, 192], replicated
- grad_gain: float32 [192], replicated
- grad_shift: float32 [192], replicated
- grad_bias: float32 [32, 6, 3312], P(('lev', 'lat'), None, 'lon')
All inputs are finite; a program needn't handle non-finite values. No bound on the sum of `lat_keep` on one device may be relied on, other than what follows from the above.
Results may differ from a plain program's by a relative error of at most 0.023.
Values may be sent and summed in bfloat16 or wider, within the bound.
A program may use at most 128 MiB of HBM per device.

v0:
```python
import math

import jax
import jax.numpy as jnp
from jax import lax
from jax.sharding import PartitionSpec as P

HEADS = 6
WZ = 2
WH = 6
WW = 12


ln_eps = 1e-05
masked_score = -1000000000.0


def from_behind(array, axis, by):
    size = lax.axis_size(axis)
    return lax.ppermute(array, axis, [(i, (i + by) % size) for i in range(size)])


def offset_table():
    span = 2 * WW - 1
    offs = jnp.arange(span)[:, None, None]
    left = jnp.arange(WW)[None, :, None]
    right = jnp.arange(WW)[None, None, :]
    return (left - right + WW - 1 == offs).astype(jnp.float32)


def expand_table(rel_table):
    groups = rel_table.shape[0]
    seven = rel_table.reshape(groups, HEADS, WZ, WZ, WH, WH, 2 * WW - 1)
    full_bias = jnp.einsum(
        "ghabcdr,rxy->ghacxbdy", seven, offset_table(), precision=lax.Precision.HIGHEST
    )
    return full_bias.reshape(groups, HEADS, WZ * WH * WW, WZ * WH * WW)


def fold_table(full_grad):
    groups = full_grad.shape[0]
    eight = full_grad.reshape(groups, HEADS, WZ, WH, WW, WZ, WH, WW)
    folded = jnp.einsum(
        "ghacxbdy,rxy->ghabcdr", eight, offset_table(), precision=lax.Precision.HIGHEST
    )
    return folded.reshape(groups, HEADS, WZ * WZ * WH * WH * (2 * WW - 1))


def window_grad(token_win, grad_win, rel_table, same_region, w_qkv, w_proj, ln_gain, ln_shift):
    groups, win_count, win_tokens, channels = token_win.shape
    head_size = channels // HEADS
    row_count = groups * win_count * win_tokens
    rows_f = token_win.reshape(row_count, channels).astype(jnp.float32)
    row_mean = jnp.mean(rows_f, -1, keepdims=True)
    centred = rows_f - row_mean
    inv_std = lax.rsqrt(jnp.mean(centred * centred, -1, keepdims=True) + ln_eps)
    x_hat = centred * inv_std
    normed = (x_hat * ln_gain + ln_shift).astype(jnp.bfloat16)
    qkv = jnp.dot(normed, w_qkv, preferred_element_type=jnp.float32).astype(jnp.bfloat16)
    head_split = qkv.reshape(groups, win_count, win_tokens, 3, HEADS, head_size)
    queries = head_split[:, :, :, 0]
    key_rows = head_split[:, :, :, 1]
    values = head_split[:, :, :, 2]
    score_scale = head_size ** (-0.5)
    scores = (
        jnp.einsum("gwihd,gwjhd->gwhij", queries, key_rows, preferred_element_type=jnp.float32)
        * score_scale
    )
    scores = scores + expand_table(rel_table)[:, None]
    scores = jnp.where(same_region[:, None, None], scores, masked_score)
    row_max = jnp.max(scores, -1, keepdims=True)
    exp_scores = jnp.exp(scores - row_max)
    attn_probs = exp_scores / jnp.sum(exp_scores, -1, keepdims=True)
    probs_b = attn_probs.astype(jnp.bfloat16)
    attended = jnp.einsum("gwhij,gwjhd->gwihd", probs_b, values, preferred_element_type=jnp.float32)
    attended = attended.astype(jnp.bfloat16).reshape(row_count, channels)
    grad_rows = grad_win.reshape(row_count, channels)
    d_wproj = jnp.dot(attended.T, grad_rows, preferred_element_type=jnp.float32)
    d_attended = jnp.dot(grad_rows, w_proj.T, preferred_element_type=jnp.float32).astype(
        jnp.bfloat16
    )
    d_attended = d_attended.reshape(groups, win_count, win_tokens, HEADS, head_size)
    d_probs = jnp.einsum(
        "gwihd,gwjhd->gwhij", d_attended, values, preferred_element_type=jnp.float32
    )
    d_values = jnp.einsum(
        "gwhij,gwihd->gwjhd", probs_b, d_attended, preferred_element_type=jnp.float32
    )
    d_values = d_values.astype(jnp.bfloat16)
    d_scores = attn_probs * (d_probs - jnp.sum(attn_probs * d_probs, -1, keepdims=True))
    d_table = fold_table(jnp.sum(d_scores, 1))
    scaled = (d_scores * score_scale).astype(jnp.bfloat16)
    d_queries = jnp.einsum(
        "gwhij,gwjhd->gwihd", scaled, key_rows, preferred_element_type=jnp.float32
    )
    d_keys = jnp.einsum("gwhij,gwihd->gwjhd", scaled, queries, preferred_element_type=jnp.float32)
    d_qkv = jnp.stack(
        [d_queries.astype(jnp.bfloat16), d_keys.astype(jnp.bfloat16), d_values], axis=3
    )
    d_qkv = d_qkv.reshape(row_count, 3 * channels)
    d_wqkv = jnp.dot(normed.T, d_qkv, preferred_element_type=jnp.float32)
    d_normed = jnp.dot(d_qkv, w_qkv.T, preferred_element_type=jnp.float32)
    d_gain = jnp.sum(d_normed * x_hat, 0)
    d_shift = jnp.sum(d_normed, 0)
    d_hat = d_normed * ln_gain
    d_rows = inv_std * (
        d_hat
        - jnp.mean(d_hat, -1, keepdims=True)
        - x_hat * jnp.mean(d_hat * x_hat, -1, keepdims=True)
    )
    d_rows = d_rows.astype(jnp.bfloat16).reshape(groups, win_count, win_tokens, channels)
    return (d_rows, d_table, d_wqkv, d_wproj, d_gain, d_shift)


def send_rim(rim_cells, axis_code, offset):
    if axis_code == 1:
        return from_behind(rim_cells, "lev", offset)
    if axis_code == 2:
        return from_behind(rim_cells, "lat", offset)
    return from_behind(rim_cells, "lon", offset)


def roll_axis(field, axis_dim, rim_width, axis_code, forward):
    extent = field.shape[axis_dim]
    if forward:
        rim_cells = lax.slice_in_dim(field, 0, rim_width, axis=axis_dim)
        arrived = send_rim(rim_cells, axis_code, -1)
        return jnp.concatenate(
            [lax.slice_in_dim(field, rim_width, extent, axis=axis_dim), arrived], axis_dim
        )
    rim_cells = lax.slice_in_dim(field, extent - rim_width, extent, axis=axis_dim)
    arrived = send_rim(rim_cells, axis_code, 1)
    return jnp.concatenate(
        [arrived, lax.slice_in_dim(field, 0, extent - rim_width, axis=axis_dim)], axis_dim
    )


def roll_grid(field, forward):
    field = roll_axis(field, 2, WZ // 2, 1, forward)
    field = roll_axis(field, 3, WH // 2, 2, forward)
    return roll_axis(field, 4, WW // 2, 3, forward)


def partition(field):
    stacks, members, levels, rows, longs, channels = field.shape
    split = field.reshape(
        stacks, members, levels // WZ, WZ, rows // WH, WH, longs // WW, WW, channels
    )
    split = split.transpose(2, 4, 0, 1, 6, 3, 5, 7, 8)
    return split.reshape(
        levels // WZ * (rows // WH), stacks, members * (longs // WW), WZ * WH * WW, channels
    )


def assemble(windows, stacks, members, levels, rows, longs):
    channels = windows.shape[-1]
    split = windows.reshape(
        levels // WZ, rows // WH, stacks, members, longs // WW, WZ, WH, WW, channels
    )
    split = split.transpose(2, 3, 0, 5, 1, 6, 4, 7, 8)
    return split.reshape(stacks, members, levels, rows, longs, channels)


def region_windows(region_ids):
    levels, rows = region_ids.shape
    split = region_ids.reshape(levels // WZ, WZ, rows // WH, WH).transpose(0, 2, 1, 3)
    split = split.reshape(levels // WZ * (rows // WH), WZ * WH)
    per_token = jnp.repeat(split, WW, axis=1)
    return per_token[:, :, None] == per_token[:, None, :]


def local(tokens, cotangent, w_qkv, w_proj, ln_gain, ln_shift, bias_table, region_ids, lat_keep):
    members, levels, rows, longs, channels = tokens.shape
    masked = cotangent * lat_keep[None, None, :, None, None].astype(jnp.bfloat16)
    stacked = roll_grid(jnp.stack([tokens, masked], 0), True)
    windows = partition(stacked)
    type_count = windows.shape[0]
    group_size = math.gcd(type_count, 4)
    loop_count = type_count // group_size
    win_shape = windows.shape[2:]
    token_windows = windows[:, 0].reshape((loop_count, group_size) + win_shape)
    grad_windows = windows[:, 1].reshape((loop_count, group_size) + win_shape)
    same_region = region_windows(region_ids)
    same_region = same_region.reshape((loop_count, group_size) + same_region.shape[1:])
    table_blocks = bias_table.reshape((loop_count, group_size) + bias_table.shape[1:])

    def block_step(sums, item):
        token_win, grad_win, rel_table, same_block = item
        d_rows, d_table, d_wqkv, d_wproj, d_gain, d_shift = window_grad(
            token_win, grad_win, rel_table, same_block, w_qkv, w_proj, ln_gain, ln_shift
        )
        sums = (sums[0] + d_wqkv, sums[1] + d_wproj, sums[2] + d_gain, sums[3] + d_shift)
        return (sums, (d_rows, d_table))

    start = (
        jnp.zeros((channels, 3 * channels), jnp.float32),
        jnp.zeros((channels, channels), jnp.float32),
        jnp.zeros((channels,), jnp.float32),
        jnp.zeros((channels,), jnp.float32),
    )
    sums, (d_windows, d_tables) = lax.scan(
        block_step, start, (token_windows, grad_windows, table_blocks, same_region)
    )
    d_windows = d_windows.reshape((type_count, 1) + win_shape)
    d_tables = d_tables.reshape(bias_table.shape)
    d_shifted = assemble(d_windows, 1, members, levels, rows, longs)
    back = roll_grid(d_shifted, False)[0]
    grad_tokens = (cotangent.astype(jnp.float32) + back.astype(jnp.float32)).astype(jnp.bfloat16)
    token_total = (
        members
        * levels
        * rows
        * longs
        * lax.axis_size("lon")
        * lax.axis_size("lev")
        * lax.axis_size("lat")
    )
    grad_scale = 1.0 / math.sqrt(token_total)
    grad_bias = lax.psum_scatter(
        d_tables.astype(jnp.bfloat16), "lon", scatter_dimension=2, tiled=True
    ).astype(jnp.float32)
    sum_qkv, sum_proj, sum_gain, sum_shift = lax.psum(
        (sums[0], sums[1], sums[2], sums[3]), ("lon", "lev", "lat")
    )
    return (
        grad_tokens,
        sum_qkv * grad_scale,
        sum_proj * grad_scale,
        sum_gain * grad_scale,
        sum_shift * grad_scale,
        grad_bias,
    )


def solution(mesh):
    placed = (
        P(None, "lev", "lat", "lon", None),
        P(None, "lev", "lat", "lon", None),
        P(),
        P(),
        P(),
        P(),
        P(("lev", "lat"), None, None),
        P("lev", "lat"),
        P("lat"),
    )
    return jax.shard_map(
        local,
        mesh=mesh,
        in_specs=placed,
        out_specs=(
            P(None, "lev", "lat", "lon", None),
            P(),
            P(),
            P(),
            P(),
            P(("lev", "lat"), None, "lon"),
        ),
        check_vma=False,
    )
```

profile of v0, /device:TPU:1, one launch (start us, length us, event | category | flops | bytes accessed | tf_op | source)
XLA Modules:
  0.0 653.4 jit_solution(11931879451814158509)
XLA Ops:
  7.9 2.0 fusion.31
  10.8 3.4 collective-permute-start
  14.2 1.8 reshape.188
  16.0 8.9 %convolution_bitcast_fusion = f32[2,6,2,6,12,2,6,12]{7,6,3,5,2,1,0,4:T(8,128)} fusion(f32[2,6,2,2,6,6,23]{6,5,4,3,2,0,1:T(8,128)S(1)} %reshape.188, s32[12,12]{1,0:T(8,128)S(1)} %subtract_add_fusion), kind=kOutput, calls=%fused_computation.2 | convolution fusion | flops 68680944 | bytes 1154880 | tf_op jit(solution)/shard_map/while/body/eval_jaxpr/ghabcdr,rxy->ghacxbdy/dot_general | solution.py:34
  24.9 20.7 %copy.147 = f32[2,6,2,6,12,2,6,12]{4,3,2,7,6,5,1,0:T(8,128)} copy(f32[2,6,2,6,12,2,6,12]{7,6,3,5,2,1,0,4:T(8,128)} %convolution_bitcast_fusion) | data formatting | bytes 1990656 | tf_op jit(solution)/shard_map/while/body/eval_jaxpr/add | solution.py:69
  45.5 10.3 %reshape.200 = f32[2,6,144,144]{2,3,1,0:T(8,128)} reshape(f32[2,6,2,6,12,2,6,12]{4,3,2,7,6,5,1,0:T(8,128)} %copy.147) | data formatting | bytes 1990656 | tf_op jit(solution)/shard_map/while/body/eval_jaxpr/add | solution.py:69
  59.4 3.3 collective-permute-done.1
  63.5 8.5 %collective-permute-start.2 = (bf16[2,2,2,12,6,192]{5,1,4,3,2,0:T(2,128)(2,1)S(1)}, bf16[2,2,2,12,6,192]{5,1,4,3,2,0:T(2,128)(2,1)S(1)}, u32[]{:S(2)}, u32[]{:S(2)}) collective-permute-start(bf16[2,2,2,12,6,192]{5,1,4,3,2,0:T(2,128)(2,1)S(1)} %get-tuple-element.65), channel_id=1, source_target_pairs={{0,240},{16,0},{32,16},{48,32},{64,48},{80,64},{96,80},{112,96},{1... | collective-permute-start | bytes 663560 | tf_op jit(solution)/shard_map/ppermute | solution.py:20
  72.1 6.6 %collective-permute-done.2 = bf16[2,2,2,12,6,192]{5,1,4,3,2,0:T(2,128)(2,1)S(1)} collective-permute-done((bf16[2,2,2,12,6,192]{5,1,4,3,2,0:T(2,128)(2,1)S(1)}, bf16[2,2,2,12,6,192]{5,1,4,3,2,0:T(2,128)(2,1)S(1)}, u32[]{:S(2)}, u32[]{:S(2)}) %collective-permute-start.2) | collective-permute-done | bytes 221216 | tf_op jit(solution)/shard_map/ppermute | solution.py:20
  81.8 1.0 reshape.190
  84.5 1.9 fusion.56
  86.4 3.5 fusion.24
  90.0 4.9 fusion.60
  94.8 2.7 fusion.14
  97.5 6.3 fusion.13
  103.8 7.0 %fusion.12 = bf16[2,2,144,1,6,32]{2,5,4,1,0,3:T(8,128)(2,1)} fusion(bf16[2,2,144,1,6,32]{2,1,0,5,4,3:T(2,128)(2,1)S(1)} %copy-done.4, f32[2,2,6,144,144]{3,4,2,1,0:T(8,128)} %fusion.24, f32[2,2,6,144,144]{3,4,2,1,0:T(8,128)} %get-tuple-element.73, f32[2,2,6,144]{3,2,1,0:T(8,128)S(1)} %get-tuple-element.72), kind=kOutput, calls=%fused_computation.23 | convolution fusion | flops 35448336 | bytes 4437504 | tf_op jit(solution)/shard_map/while/body/eval_jaxpr/gwhij,gwjhd->gwihd/dot_general | solution.py:93
  111.1 3.3 fusion.15
  115.3 2.3 fusion.61
  117.9 1.4 copy.132
  121.4 1.1 fusion.59
  122.5 1.2 fusion.62
  125.3 10.1 %reshape.201 = f32[2,6,2,6,12,2,6,12]{4,3,2,7,6,5,1,0:T(8,128)} reshape(f32[2,6,144,144]{2,3,1,0:T(8,128)} %fusion.61) | data formatting | bytes 1990656 | tf_op jit(solution)/shard_map/while/body/eval_jaxpr/reshape | solution.py:42
  135.5 20.1 %copy.138 = f32[2,6,2,6,12,2,6,12]{7,6,4,5,3,2,1,0:T(8,128)} copy(f32[2,6,2,6,12,2,6,12]{4,3,2,7,6,5,1,0:T(8,128)} %reshape.201) | data formatting | bytes 1990656 | tf_op jit(solution)/shard_map/while/body/eval_jaxpr/reshape | solution.py:42
  155.5 13.1 %fusion.11 = bf16[2,6,2,2,6,6,23]{6,5,3,4,2,1,0:T(8,128)(2,1)S(1)} fusion(f32[2,6,2,6,12,2,6,12]{7,6,4,5,3,2,1,0:T(8,128)} %copy.138, s32[12,12]{1,0:T(8,128)S(1)} %subtract_add_fusion), kind=kOutput, calls=%fused_computation.18 | convolution fusion | flops 68720688 | bytes 1075392 | tf_op jit(solution)/shard_map/while/body/eval_jaxpr/ghacxbdy,rxy->ghabcdr/dot_general | solution.py:43
  168.6 77.8 %all-reduce.1 = (f32[192]{0:T(256)S(1)}, f32[192]{0:T(256)S(1)}) all-reduce(f32[192]{0:T(256)S(1)} %get-tuple-element.36, f32[192]{0:T(256)S(1)} %get-tuple-element.39), channel_id=1, replica_groups=mesh['lon'=16,'lev'=4,'lat'=4] {'lon','lev','lat'}, use_global_device_ids=true, to_apply=%region_10.11 | all-reduce | flops 384 | bytes 3072 | tf_op jit(solution)/shard_map/psum | solution.py:222
  247.1 1.3 convert_element_type.126
  251.4 126.8 %all-reduce.6.cloned.1.call-done = bf16[2,6,3312]{2,0,1:T(2,128)(2,1)} async-done(((bf16[2,6,3312]{2,0,1:T(2,128)(2,1)}), bf16[2,6,3312]{2,0,1:T(2,128)(2,1)}) %all-reduce.6.cloned.1.call-update) | async-done | bytes 79504
  378.2 1.4 dynamic-slice_convert_fusion
  379.6 1.1 fusion.20
  380.7 262.1 %all-reduce.8.cloned.1.call-done = (f32[192,576]{1,0:T(8,128)}, f32[192,192]{1,0:T(8,128)}) async-done(((f32[192,576]{1,0:T(8,128)}, f32[192,192]{1,0:T(8,128)}), (f32[192,576]{1,0:T(8,128)}, f32[192,192]{1,0:T(8,128)})) %all-reduce.8.cloned.1.call-update) | async-done | bytes 589840 | tf_op jit(solution)/shard_map/psum | solution.py:222
  642.9 1.9 broadcast_multiply_fusion
  644.7 1.6 broadcast_multiply_fusion.1
  (88 shorter events, 18.9 us)
Async XLA Ops:
  7.2 75.7 %copy-start = (bf16[192,576]{1,0:T(8,128)(2,1)S(1)}, bf16[192,576]{1,0:T(8,128)(2,1)}, u32[]{:S(2)}) copy-start(bf16[192,576]{1,0:T(8,128)(2,1)} %param.11) | copy-start | bytes 663556
  7.2 371.0 %all-reduce.6.cloned.1.call-start = ((), (), s32[]{:S(2)}) async-start(), calls=%async_computation | async-start | bytes 159744
  10.8 46.5 %collective-permute-start = (bf16[2,2,1,12,12,192]{5,1,4,3,2,0:T(2,128)(2,1)S(1)}, bf16[2,2,1,12,12,192]{5,1,4,3,2,0:T(2,128)(2,1)S(1)}, u32[]{:S(2)}, u32[]{:S(2)}) collective-permute-start(bf16[2,2,1,12,12,192]{5,1,4,3,2,0:T(2,128)(2,1)S(1)} %get-tuple-element.67), channel_id=1, source_target_pairs={{0,12},{4,0},{8,4},{12,8},{1,13},{5,1},{9,5},{13,9},{2,14},{6,2},{... | collective-permute-start | bytes 663560 | tf_op jit(solution)/shard_map/ppermute | solution.py:20
  45.5 10.3 %copy-start.11 = (s32[2,12]{1,0:T(2,128)S(1)}, s32[2,12]{1,0:T(2,128)}, u32[]{:S(2)}) copy-start(s32[2,12]{1,0:T(2,128)} %param.16) | copy-start | bytes 292
  45.5 10.6 %copy-start.12 = (u32[256]{0:T(256)S(1)}, u32[256]{0:T(256)}, u32[]{:S(2)}) copy-start(u32[256]{0:T(256)} %constant.59) | copy-start | bytes 3076
  57.6 5.0 collective-permute-start.1
  63.5 18.0 %copy-start.8 = (bf16[192,192]{1,0:T(8,128)(2,1)S(1)}, bf16[192,192]{1,0:T(8,128)(2,1)}, u32[]{:S(2)}) copy-start(bf16[192,192]{1,0:T(8,128)(2,1)} %param.12) | copy-start | bytes 221188
  63.5 15.2 %collective-permute-start.2 = (bf16[2,2,2,12,6,192]{5,1,4,3,2,0:T(2,128)(2,1)S(1)}, bf16[2,2,2,12,6,192]{5,1,4,3,2,0:T(2,128)(2,1)S(1)}, u32[]{:S(2)}, u32[]{:S(2)}) collective-permute-start(bf16[2,2,2,12,6,192]{5,1,4,3,2,0:T(2,128)(2,1)S(1)} %get-tuple-element.65), channel_id=1, source_target_pairs={{0,240},{16,0},{32,16},{48,32},{64,48},{80,64},{96,80},{112,96},{1... | collective-permute-start | bytes 663560 | tf_op jit(solution)/shard_map/ppermute | solution.py:20
  79.6 3.3 copy-start.9
  79.6 3.3 copy-start.10
  86.4 3.5 copy-start.4
  86.4 3.5 copy-start.5
  90.0 4.9 copy-start.2
  111.0 3.3 copy-start.1
  111.0 4.3 copy-start.13
  115.3 2.3 copy-start.6
  120.1 3.7 copy-start.7
  122.5 125.9 %collective-permute-start.3 = (bf16[1,2,1,12,12,192]{5,2,4,3,1,0:T(2,128)(2,1)}, bf16[1,2,1,12,12,192]{5,2,4,3,1,0:T(2,128)(2,1)S(1)}, u32[]{:S(2)}, u32[]{:S(2)}) collective-permute-start(bf16[1,2,1,12,12,192]{5,2,4,3,1,0:T(2,128)(2,1)} %get-tuple-element.70), channel_id=1, source_target_pairs={{0,4},{4,8},{8,12},{12,0},{1,5},{5,9},{9,13},{13,1},{2,6},{6,10},{... | collective-permute-start | bytes 331784 | tf_op jit(solution)/shard_map/ppermute | solution.py:20
  168.6 211.0 %copy-start.3 = (bf16[2,2,12,12,192]{4,1,3,2,0:T(2,128)(2,1)S(1)}, bf16[2,2,12,12,192]{4,1,3,2,0:T(2,128)(2,1)}, u32[]{:S(2)}) copy-start(bf16[2,2,12,12,192]{4,1,3,2,0:T(2,128)(2,1)} %param.10) | copy-start | bytes 663556
  248.4 394.5 %all-reduce.8.cloned.1.call-start = ((), (), s32[]{:S(2)}) async-start(), calls=%async_computation.1 | async-start | bytes 1376256 | tf_op jit(solution)/shard_map/psum | solution.py:222
  248.6 1.8 collective-permute-start.4
  251.3 128.3 %collective-permute-start.5 = (bf16[1,2,2,12,6,192]{5,2,4,3,1,0:T(2,128)(2,1)S(1)}, bf16[1,2,2,12,6,192]{5,2,4,3,1,0:T(2,128)(2,1)S(1)}, u32[]{:S(2)}, u32[]{:S(2)}) collective-permute-start(bf16[1,2,2,12,6,192]{5,2,4,3,1,0:T(2,128)(2,1)S(1)} %get-tuple-element.68), channel_id=1, source_target_pairs={{0,16},{16,32},{32,48},{48,64},{64,80},{80,96},{96,112},{112,128},... | collective-permute-start | bytes 331784 | tf_op jit(solution)/shard_map/ppermute | solution.py:20
Sparse Core Ops, SparseCore 0:
  248.5 129.6 all-reduce.5
  385.3 257.5 all-reduce.7
where the time goes:
time: 663 us; the launch traced here: 653 us
  waiting for transfers between devices  400 us (60%)
  blocking collectives  77.8 us (12%)
  local copies, waits for them, and re-layouts  76.2 us (11%)
  matrix products  53 us (8%)
  other arithmetic  17.8 us (3%)
  between operations  15.3 us (2%)
  starting transfers between devices  13.5 us (2%)
    psum x1, waiting for transfers between devices, local(): lax.psum((sums[0], sums[1], sums[2], sums[3]), ('lon', 'lev', 'lat'))  262 us
    unnamed x3, waiting for transfers between devices  127 us
    psum x1, blocking collectives, local(): lax.psum((sums[0], sums[1], sums[2], sums[3]), ('lon', 'lev', 'lat'))  77.8 us
    add x2, local copies, waits for them, and re-layouts, window_grad(): scores = scores + expand_table(rel_table)[:, None]  30.9 us
    reshape x2, local copies, waits for them, and re-layouts, fold_table(): eight = full_grad.reshape(groups, HEADS, WZ, WH, WW, WZ, WH, WW)  30.2 us
    ppermute x6, starting transfers between devices, from_behind(): lax.ppermute(array, axis, [(i, (i + by) % size) for i in range(size)])  13.4 us
  transfers between devices with their start and end apart: 8, of which 5 were waited for; matrix products, arithmetic and copies ran while one was open for 15% of the time, Pallas kernels for 0%

commit v1 on v0

v1 whole, which is shorter than its diff:
```python
import math

import jax
import jax.numpy as jnp
import numpy as np
from jax import lax
from jax.experimental import pallas as pl
from jax.experimental.pallas import tpu as pltpu
from jax.sharding import PartitionSpec as P

MESH = pl.DeviceIdType.MESH
F32 = jnp.float32
BF16 = jnp.bfloat16

HEADS = 6
WZ = 2
WH = 6
WW = 12
MEMBERS = 2
LEVELS = 2
ROWS = 12
LONGS = 12
C = 192
DH = C // HEADS
WIN = WZ * WH * WW
TYPES = 2
TOKENS = MEMBERS * LEVELS * ROWS * LONGS
SPAN = 2 * WW - 1
FOLD = WH * SPAN
PIECES = 640
MASKED = -1000000000.0
EPS = 1e-05

PIECE_AT = [0, 112, 224, 336, 448, 496, 544, 592]
PIECE_LEN = [112, 112, 112, 112, 48, 48, 48, 48]
BLOCKS = 13


def piece_steps(q):
    return (q // 2) % 2, q // 4, q % 2


def index_rows():
    out = np.full((16, PIECES), -1, np.int32)
    of_natural = np.full(PIECES, -1, np.int32)
    of_window = np.full(PIECES, -1, np.int32)
    for q in range(8):
        dz, dh, dw = piece_steps(q)
        rows = 3 if dh else 9
        for m in range(MEMBERS):
            for hh in range(rows):
                for ww in range(6):
                    s = PIECE_AT[q] + (m * rows + hh) * 6 + ww
                    lev = 1 - dz
                    row = hh if dh else 3 + hh
                    lon = ww if dw else 6 + ww
                    of_natural[s] = ((m * LEVELS + lev) * ROWS + row) * LONGS + lon
                    there = 9 + hh if dh else hh
                    t, h = there // WH, there % WH
                    w = 6 + ww if dw else ww
                    of_window[s] = (t * MEMBERS + m) * WIN + w * 12 + dz * WH + h
    out[0] = of_natural
    out[3] = of_window
    for s in range(PIECES):
        if of_natural[s] >= 0:
            out[2, of_natural[s]] = s
            out[1, of_window[s]] = s
    for rr in range(SPAN):
        for zj in range(WZ):
            for hj in range(WH):
                out[4, (rr * WZ + zj) * WH + hj] = zj * 256 + hj * SPAN + SPAN - 1 - rr
    for b in range(12):
        for t in range(TYPES):
            for h in range(HEADS):
                th, slot = t * HEADS + h, t * 8 + h
                out[5, b * 16 + slot] = th * 16 + b
                out[6, th * 16 + b] = b * 16 + slot
    for zj in range(WZ):
        for hj in range(WH):
            for r in range(SPAN):
                src = ((SPAN - 1 - r) * WZ + zj) * WH + hj
                flat = hj * SPAN + r
                out[7 + zj, flat] = src
                if hj < 3:
                    out[9 + zj, FOLD + flat] = src
                else:
                    out[11 + zj, flat - FOLD // 2] = src
                out[13 + zj, FOLD // 2 + flat] = src
    out[15, :384] = np.arange(384) % 12
    return out


def dot(a, b):
    return lax.dot_general(a, b, (((1,), (0,)), ((), ())), preferred_element_type=F32)


def dot_nt(a, b):
    return lax.dot_general(a, b, (((1,), (1,)), ((), ())), preferred_element_type=F32)


def dot_tn(a, b):
    return lax.dot_general(a, b, (((0,), (0,)), ((), ())), preferred_element_type=F32)


def make_body(lon_n, lev_n, lat_n):
    z_n = lon_n // 2
    y_n = lat_n // 2
    plane_n = 2 * y_n * lev_n
    total = MEMBERS * LEVELS * ROWS * LONGS * lon_n * lev_n * lat_n
    grad_scale = 1.0 / math.sqrt(total)
    score_scale = DH ** (-0.5)

    def body(
        tok, cot, wqkv, wproj, gain, shift, table, reg, keep, idx,
        out_tok, out_qkv, out_proj, out_gain, out_shift, out_bias,
        ztok, zcot, sbuf, rbuf, xt, xg, dx, sb2, rb2,
        xk, bm, dacc, w3, wt, pw, pwt, pnt, qkvt, dqt, ot,
        accq, accp, accs, payf, payb, pairb, rsrc, plb, zbuf, fbuf, bmsg, brcv,
        s_h, r_h, s_o, r_o, s_p, r_p, s_1, r_1, s_2, r_2, s_3, r_3, s_4, r_4, s_b, r_b,
    ):
        o = lax.axis_index("lon")
        lv = lax.axis_index("lev")
        la = lax.axis_index("lat")
        core = lax.rem(la, 2)
        ylo = lax.div(la, 2)
        zz = lax.rem(o, z_n)
        yhi = lax.div(o, z_n)
        me_p = (yhi * y_n + ylo) * lev_n + lv

        def halo_dev(q, sign):
            dz, dh, dw = piece_steps(q)
            return {
                "lon": lax.rem(o + sign * dw + lon_n, lon_n),
                "lev": lax.rem(lv + sign * dz + lev_n, lev_n),
                "lat": lax.rem(la + sign * dh + lat_n, lat_n),
            }

        def plane_dev(p):
            ph = lax.div(p, y_n * lev_n)
            rest = lax.rem(p, y_n * lev_n)
            return {
                "lon": ph * z_n + zz,
                "lev": lax.rem(rest, lev_n),
                "lat": lax.div(rest, lev_n) * 2 + core,
            }

        def z_dev(k):
            return {"lon": yhi * z_n + lax.rem(zz + k, z_n), "lev": lv, "lat": la}

        def lon_dev(k):
            return {"lon": lax.rem(o + k, lon_n), "lev": lv, "lat": la}

        pair_dev = {"lon": o, "lev": lv, "lat": ylo * 2 + 1 - core}

        def remote(src, dst, ssem, rsem, dev):
            return pltpu.make_async_remote_copy(
                src_ref=src, dst_ref=dst, send_sem=ssem, recv_sem=rsem,
                device_id=dev, device_id_type=MESH,
            )

        partners = [halo_dev(q, s) for q in range(1, 8) for s in (-1, 1)]
        partners.append(pair_dev)
        partners += [plane_dev(lax.rem(me_p + k, plane_n)) for k in range(1, plane_n)]
        partners += [lon_dev(k) for k in range(1, lon_n)]
        barrier = pltpu.get_barrier_semaphore()
        for dev in partners:
            pl.semaphore_signal(barrier, inc=1, device_id=dev, device_id_type=MESH)

        def onehot(row, height, width):
            pick = lax.broadcasted_iota(jnp.int32, (height, width), 0) == idx[row : row + 1, 0:width]
            return jnp.where(pick, 1.0, 0.0).astype(BF16)

        for k in range(TOKENS // 24):
            for half in range(2):
                slab = 2 * k + half
                at = 24 * k + 12 * half
                ztok[at : at + 12, :] = tok[slab].astype(F32)
                kept = keep[0, slab % ROWS].astype(F32)
                zcot[at : at + 12, :] = cot[slab].astype(F32) * kept
        gather = onehot(2, PIECES, TOKENS)
        piece_tok = dot(gather, ztok[...].astype(BF16))
        piece_cot = dot(gather, zcot[...].astype(BF16))
        sbuf[...] = jnp.concatenate([piece_tok, piece_cot], axis=1).astype(BF16)

        pl.semaphore_wait(barrier, len(partners))
        halo = []
        for q in range(1, 8):
            part = pl.ds(PIECE_AT[q], PIECE_LEN[q])
            copy = remote(sbuf.at[part], rbuf.at[part], s_h.at[q], r_h.at[q], halo_dev(q, -1))
            copy.start()
            halo.append(copy)
        rbuf[0:112, :] = sbuf[0:112, :]

        dacc[...] = jnp.zeros_like(dacc)
        accq[...] = jnp.zeros_like(accq)
        accp[...] = jnp.zeros_like(accp)
        accs[...] = jnp.zeros_like(accs)
        xk[...] = jnp.zeros_like(xk)
        for zi in range(WZ):
            for zj in range(WZ):
                for hi in range(WH):
                    kappa = (zi * WZ + zj) * WH + hi
                    b = zi * WH + hi
                    for t in range(TYPES):
                        xk[b * 16 + t * 8 : b * 16 + t * 8 + 6, zj * 256 : zj * 256 + FOLD] = table[
                            t, :, kappa * FOLD : (kappa + 1) * FOLD
                        ]
        to_th = onehot(5, 192, 192)
        to_lane = onehot(4, 512, 384)
        rest = xk[...]
        wide = jnp.zeros((192, 384), F32)
        for _ in range(3):
            term = rest.astype(BF16)
            rest = rest - term.astype(F32)
            wide = wide + dot(dot(to_th, term).astype(BF16), to_lane)
        lane_a = idx[15:16, 0:384]
        row_b = lax.broadcasted_iota(jnp.int32, (16, 384), 0)
        masked = []
        for t in range(TYPES):
            reg_a = jnp.zeros((16, 384), jnp.int32)
            reg_b = jnp.zeros((16, 384), jnp.int32)
            for z in range(WZ):
                for h in range(WH):
                    ident = reg[z, t * WH + h]
                    reg_a = jnp.where(lane_a == z * WH + h, ident, reg_a)
                    reg_b = jnp.where(row_b == z * WH + h, ident, reg_b)
            for h in range(HEADS):
                th = t * HEADS + h
                masked.append(jnp.where(reg_a == reg_b, wide[th * 16 : th * 16 + 16], MASKED))
        wide = jnp.concatenate(masked, axis=0)
        for x in range(WW):
            moved = pltpu.roll(wide, (384 - 12 * (WW - 1 - x)) % 384, 1) if x < WW - 1 else wide
            for th in range(TYPES * HEADS):
                bm[th, 12 * x : 12 * x + 12, :] = moved[16 * th : 16 * th + 12, 0:WIN]
        for part in range(3):
            w3[part] = wqkv[:, part * C : (part + 1) * C]
        wt[...] = wqkv[...].astype(F32).T.astype(BF16)
        to_window = onehot(3, TOKENS, PIECES)
        pwt[...] = onehot(1, PIECES, TOKENS)
        pnt[...] = onehot(0, TOKENS, PIECES)

        for copy in halo:
            copy.wait_recv()
        arrived = dot(to_window, rbuf[...])
        xt[...] = arrived[:, 0:C]
        xg[...] = arrived[:, C : 2 * C].astype(BF16)

        head_of = lax.broadcasted_iota(jnp.int32, (1, C), 1) // DH
        eye = jnp.where(
            lax.broadcasted_iota(jnp.int32, (C, C), 0) == lax.broadcasted_iota(jnp.int32, (C, C), 1),
            1.0, 0.0,
        ).astype(BF16)

        def window(w, carry):
            r0 = pl.multiple_of(w * WIN, 16)
            t = lax.div(w, MEMBERS)
            x = xt[pl.ds(r0, WIN), :]
            g = xg[pl.ds(r0, WIN), :]
            centred = x - jnp.mean(x, axis=1, keepdims=True)
            inv_std = lax.rsqrt(jnp.mean(centred * centred, axis=1, keepdims=True) + EPS)
            x_hat = centred * inv_std
            normed = (x_hat * gain[...] + shift[...]).astype(BF16)
            q = dot(normed, w3[0]).astype(BF16)
            k = dot(normed, w3[1]).astype(BF16)
            v = dot(normed, w3[2]).astype(BF16)
            d_att = dot_nt(g, wproj[...]).astype(BF16)
            qkvt[0 : 3 * C, :] = dot_nt(wt[...], normed).astype(BF16)
            qkvt[3 * C : 4 * C, :] = dot_nt(wproj[...], g).astype(BF16)
            for h in range(HEADS):
                th = t * HEADS + h
                mine = head_of == h
                zero = jnp.zeros_like(q)
                s = dot_nt(jnp.where(mine, q, zero), k) * score_scale + bm[th]
                e = jnp.exp(s - jnp.max(s, axis=1, keepdims=True))
                p = e * (1.0 / jnp.sum(e, axis=1, keepdims=True))
                pb = p.astype(BF16)
                d_p = dot_nt(jnp.where(mine, d_att, zero), v)
                lo = h * DH
                ot[lo : lo + DH, :] = dot_nt(qkvt[2 * C + lo : 2 * C + lo + DH, :], pb).astype(BF16)
                dqt[2 * C + lo : 2 * C + lo + DH, :] = dot(
                    qkvt[3 * C + lo : 3 * C + lo + DH, :], pb
                ).astype(BF16)
                ds = p * (d_p - jnp.sum(p * d_p, axis=1, keepdims=True))
                at = pl.multiple_of(th * 16, 16)
                for xx in range(WW):
                    dacc[xx, pl.ds(at, 12), :] += ds[12 * xx : 12 * xx + 12, :]
                sc = (ds * score_scale).astype(BF16)
                dqt[lo : lo + DH, :] = dot_nt(qkvt[C + lo : C + lo + DH, :], sc).astype(BF16)
                dqt[C + lo : C + lo + DH, :] = dot(qkvt[lo : lo + DH, :], sc).astype(BF16)
            accp[...] += dot(ot[...], g)
            accq[...] += dot_nt(dot_nt(eye, normed).astype(BF16), dqt[...])
            d_normed = dot_tn(dqt[...], wt[...])
            accs[0:1, :] += jnp.sum(d_normed * x_hat, axis=0, keepdims=True)
            accs[1:2, :] += jnp.sum(d_normed, axis=0, keepdims=True)
            d_hat = d_normed * gain[...]
            m1 = jnp.mean(d_hat, axis=1, keepdims=True)
            m2 = jnp.mean(d_hat * x_hat, axis=1, keepdims=True)
            dx[pl.ds(r0, WIN), :] = (inv_std * (d_hat - m1 - x_hat * m2)).astype(BF16)
            return carry

        lax.fori_loop(0, TYPES * MEMBERS, window, 0)

        payf[...] = jnp.zeros_like(payf)
        payf[0, 0:C, :] = accq[:, 0:384]
        payf[1, 0:C, :] = jnp.concatenate([accq[:, 384:576], accp[...]], axis=1)
        payf[0, C : C + 8, 0:C] = accs[...]
        payb[...] = payf[...].astype(BF16)
        pair = remote(payb.at[1 - core], pairb, s_p, r_p, pair_dev)
        pair.start()

        sb2[...] = dot(pwt[...], dx[...]).astype(BF16)
        back = []
        for q in range(1, 8):
            part = pl.ds(PIECE_AT[q], PIECE_LEN[q])
            copy = remote(sb2.at[part], rb2.at[part], s_o.at[q], r_o.at[q], halo_dev(q, 1))
            copy.start()
            back.append(copy)
        rb2[0:112, :] = sb2[0:112, :]

        pair.wait_recv()
        rsrc[...] = (payf[core] + pairb[...].astype(F32)).astype(BF16)

        def block(ref, p):
            return ref.at[pl.ds(pl.multiple_of(p * 16, 16), 16)]

        def plane_copy(k):
            p = lax.rem(me_p + k, plane_n)
            return p, remote(
                block(rsrc, p), plb.at[k], s_1.at[k], r_1.at[k], plane_dev(p)
            )

        for k in range(1, plane_n):
            p, copy = plane_copy(k)
            pl.when(p < BLOCKS)(copy.start)

        folded = jnp.zeros((192, 384), F32)
        for x in range(WW):
            padded = jnp.concatenate([dacc[x], jnp.zeros((192, 384 - WIN), F32)], axis=1)
            off = 12 * (WW - 1 - x)
            folded = folded + (pltpu.roll(padded, off, 1) if off else padded)
        by_b = dot(onehot(6, 192, 192), folded.astype(BF16)).astype(BF16)
        for zj in range(WZ):
            pa, pb2, pc, pd = [dot(by_b, onehot(row + zj, 384, 256)) for row in (7, 9, 11, 13)]
            for zi in range(WZ):
                for u in range(2):
                    d = ((zi * WZ + zj) * 2 + u) * 2
                    b0 = (zi * WH + 3 * u) * 16
                    bmsg[d] = (pa[b0 : b0 + 16] + pb2[b0 + 16 : b0 + 32]).astype(BF16)
                    bmsg[d + 1] = (pc[b0 + 16 : b0 + 32] + pd[b0 + 32 : b0 + 48]).astype(BF16)
        bias = []
        for k in range(1, lon_n):
            dev = lon_dev(k)
            copy = remote(bmsg.at[dev["lon"]], brcv.at[k], s_b.at[k], r_b.at[k], dev)
            copy.start()
            bias.append(copy)

        def z_copy(k):
            return remote(zbuf.at[zz], zbuf.at[zz], s_2.at[k], r_2.at[k], z_dev(k))

        def z_from(k):
            z = lax.rem(zz + z_n - k, z_n)
            return remote(zbuf.at[z], zbuf.at[z], s_2.at[k], r_2.at[k], z_dev(k))

        @pl.when(me_p < BLOCKS)
        def _():
            part = rsrc[pl.ds(pl.multiple_of(me_p * 16, 16), 16), :].astype(F32)
            for k in range(1, plane_n):
                remote(block(rsrc, me_p), plb.at[k], s_1.at[k], r_1.at[k], pair_dev).wait_recv()
                part = part + plb[k].astype(F32)
            zbuf[zz] = part.astype(BF16)
            for k in range(1, z_n):
                z_copy(k).start()

        for copy in back:
            copy.wait_recv()
        ztok[...] = dot(pnt[...], rb2[...])
        for k in range(TOKENS // 24):
            for half in range(2):
                slab = 2 * k + half
                at = 24 * k + 12 * half
                out_tok[slab] = (cot[slab].astype(F32) + ztok[at : at + 12, :]).astype(BF16)

        def gather_copy(k):
            p = lax.rem(me_p + k, plane_n)
            mine = block(fbuf.at[core], me_p)
            return remote(mine, mine, s_3.at[k], r_3.at[k], plane_dev(p))

        def pair_copy(k, p, side):
            there = block(fbuf.at[side], p)
            return remote(there, there, s_4.at[k], r_4.at[k], pair_dev)

        @pl.when(me_p < BLOCKS)
        def _():
            for k in range(1, z_n):
                z_from(k).wait_recv()
            part = zbuf[0].astype(F32)
            for k in range(1, z_n):
                part = part + zbuf[k].astype(F32)
            fbuf[core, pl.ds(pl.multiple_of(me_p * 16, 16), 16), :] = (part * grad_scale).astype(BF16)
            for k in range(1, plane_n):
                gather_copy(k).start()
            pair_copy(0, me_p, core).start()

        sums = bmsg[o].astype(F32)
        for k in range(1, lon_n):
            bias[k - 1].wait_recv()
            sums = sums + brcv[k].astype(F32)
        for t in range(TYPES):
            out_bias[t] = sums[8 * t : 8 * t + 6, 0 : FOLD * 3 // 2]

        for k in range(1, plane_n):
            p = lax.rem(me_p + plane_n - k, plane_n)

            @pl.when(p < BLOCKS)
            def _():
                here = block(fbuf.at[core], p)
                remote(here, here, s_3.at[k], r_3.at[k], pair_dev).wait_recv()
                pair_copy(k, p, core).start()

        for k in range(plane_n):
            p = lax.rem(me_p + plane_n - k, plane_n)

            @pl.when(p < BLOCKS)
            def _():
                pair_copy(k, p, 1 - core).wait_recv()

        out_qkv[:, 0:384] = fbuf[0, 0:C, :].astype(F32)
        right = fbuf[1, 0:C, :].astype(F32)
        out_qkv[:, 384:576] = right[:, 0:C]
        out_proj[...] = right[:, C : 2 * C]
        norms = fbuf[0, C : C + 16, :].astype(F32)
        out_gain[...] = norms[0:1, 0:C]
        out_shift[...] = norms[1:2, 0:C]

        for copy in halo + back + bias:
            copy.wait_send()
        pair.wait_send()
        for k in range(1, plane_n):
            p, copy = plane_copy(k)
            pl.when(p < BLOCKS)(copy.wait_send)

        @pl.when(me_p < BLOCKS)
        def _():
            for k in range(1, z_n):
                z_copy(k).wait_send()
            for k in range(1, plane_n):
                gather_copy(k).wait_send()

        for k in range(plane_n):
            p = lax.rem(me_p + plane_n - k, plane_n)

            @pl.when(p < BLOCKS)
            def _():
                pair_copy(k, p, core).wait_send()

    sems = pltpu.SemaphoreType.DMA
    scratch = [
        pltpu.VMEM((TOKENS, C), F32),
        pltpu.VMEM((TOKENS, C), F32),
        pltpu.VMEM((PIECES, 2 * C), BF16),
        pltpu.VMEM((PIECES, 2 * C), BF16),
        pltpu.VMEM((TOKENS, C), F32),
        pltpu.VMEM((TOKENS, C), BF16),
        pltpu.VMEM((TOKENS, C), BF16),
        pltpu.VMEM((PIECES, C), BF16),
        pltpu.VMEM((PIECES, C), BF16),
        pltpu.VMEM((192, 512), F32),
        pltpu.VMEM((TYPES * HEADS, WIN, WIN), F32),
        pltpu.VMEM((WW, 192, WIN), F32),
        pltpu.VMEM((3, C, C), BF16),
        pltpu.VMEM((3 * C, C), BF16),
        pltpu.VMEM((16, 128), BF16),
        pltpu.VMEM((PIECES, TOKENS), BF16),
        pltpu.VMEM((TOKENS, PIECES), BF16),
        pltpu.VMEM((4 * C, WIN), BF16),
        pltpu.VMEM((3 * C, WIN), BF16),
        pltpu.VMEM((C, WIN), BF16),
        pltpu.VMEM((C, 3 * C), F32),
        pltpu.VMEM((C, C), F32),
        pltpu.VMEM((8, C), F32),
        pltpu.VMEM((2, 16 * BLOCKS, 384), F32),
        pltpu.VMEM((2, 16 * BLOCKS, 384), BF16),
        pltpu.VMEM((16 * BLOCKS, 384), BF16),
        pltpu.VMEM((16 * BLOCKS, 384), BF16),
        pltpu.VMEM((plane_n, 16, 384), BF16),
        pltpu.VMEM((z_n, 16, 384), BF16),
        pltpu.VMEM((2, 16 * BLOCKS, 384), BF16),
        pltpu.VMEM((16, 16, 256), BF16),
        pltpu.VMEM((16, 16, 256), BF16),
        sems((8,)), sems((8,)), sems((8,)), sems((8,)), sems, sems,
        sems((plane_n,)), sems((plane_n,)), sems((z_n,)), sems((z_n,)),
        sems((plane_n,)), sems((plane_n,)), sems((plane_n,)), sems((plane_n,)),
        sems((lon_n,)), sems((lon_n,)),
    ]
    return body, scratch


def solution(mesh):
    lon_n, lev_n, lat_n = (mesh.shape[name] for name in ("lon", "lev", "lat"))
    body, scratch = make_body(lon_n, lev_n, lat_n)
    index = index_rows()

    def local(tokens, cotangent, w_qkv, w_proj, ln_gain, ln_shift, bias_table, region_ids, lat_keep):
        slabs = (MEMBERS * LEVELS * ROWS, LONGS, C)
        vmem = pl.BlockSpec(memory_space=pltpu.VMEM)
        smem = pl.BlockSpec(memory_space=pltpu.SMEM)
        back, g_qkv, g_proj, g_gain, g_shift, g_bias = pl.pallas_call(
            body,
            out_shape=(
                jax.ShapeDtypeStruct(slabs, BF16),
                jax.ShapeDtypeStruct((C, 3 * C), F32),
                jax.ShapeDtypeStruct((C, C), F32),
                jax.ShapeDtypeStruct((1, C), F32),
                jax.ShapeDtypeStruct((1, C), F32),
                jax.ShapeDtypeStruct((TYPES, HEADS, FOLD * 3 // 2), F32),
            ),
            in_specs=[vmem] * 7 + [smem, smem, vmem],
            out_specs=(vmem,) * 6,
            scratch_shapes=scratch,
            compiler_params=pltpu.CompilerParams(
                collective_id=0, has_side_effects=True, vmem_limit_bytes=56 * 1024 * 1024
            ),
        )(
            tokens.reshape(slabs), cotangent.reshape(slabs), w_qkv, w_proj,
            ln_gain.reshape(1, C), ln_shift.reshape(1, C), bias_table,
            region_ids, lat_keep.reshape(1, ROWS), jnp.asarray(index),
        )
        return (
            back.reshape(tokens.shape), g_qkv, g_proj, g_gain.reshape(C), g_shift.reshape(C), g_bias,
        )

    return jax.shard_map(
        local,
        mesh=mesh,
        in_specs=(
            P(None, "lev", "lat", "lon", None),
            P(None, "lev", "lat", "lon", None),
            P(), P(), P(), P(),
            P(("lev", "lat"), None, None),
            P("lev", "lat"),
            P("lat"),
        ),
        out_specs=(
            P(None, "lev", "lat", "lon", None),
            P(), P(), P(), P(),
            P(("lev", "lat"), None, "lon"),
        ),
        check_vma=False,
    )
```

time: 663 us -> 69.1 us (0.10); the launches traced: 653 us -> 68.9 us
  waiting for transfers between devices: 400 us -> 0 us
  blocking collectives: 77.8 us -> 0 us
  local copies, waits for them, and re-layouts: 76.2 us -> 9.18 us
  Pallas kernels: 0 us -> 59 us
  matrix products: 53 us -> 0 us
  other arithmetic: 17.8 us -> 0 us
  between operations: 15.3 us -> 0.67 us
  starting transfers between devices: 13.5 us -> 0 us
    psum x1 -> x0, waiting for transfers between devices: 262 us -> none  [local(): lax.psum((sums[0], sums[1], sums[2], sums[3]), ('lon', 'lev', 'lat'))]
    unnamed x3 -> x0, waiting for transfers between devices: 127 us -> none
    psum x1 -> x0, blocking collectives: 77.8 us -> none  [local(): lax.psum((sums[0], sums[1], sums[2], sums[3]), ('lon', 'lev', 'lat'))]
    pallas_call x0 -> x1, Pallas kernels: none -> 59 us  [local(): pl.pallas_call(body, out_shape=(jax.ShapeDtypeStruct(slabs, BF16), jax.Sh...]
    dot_general x12 -> x0, matrix products: 48.2 us -> none  [the longest x1 13.1 us: fold_table(): jnp.einsum('ghacxbdy,rxy->ghabcdr', eight, offset_table(), precision=lax....]
    reshape x10 -> x0, local copies, waits for them, and re-layouts: 35.4 us -> none  [the longest x2 30.2 us: fold_table(): eight = full_grad.reshape(groups, HEADS, WZ, WH, WW, WZ, WH, WW)]
    add x2 -> x0, local copies, waits for them, and re-layouts: 30.9 us -> none  [window_grad(): scores = scores + expand_table(rel_table)[:, None]]
    ppermute x6 -> x0, starting transfers between devices: 13.4 us -> none  [from_behind(): lax.ppermute(array, axis, [(i, (i + by) % size) for i in range(size)])]
  transfers between devices with their start and end apart: 8 -> 0, of which waited for: 5 -> 0; matrix products, arithmetic and copies ran while one was open for 15% -> 0% of each run, Pallas kernels for 0% -> 0%
where the time goes in v1:
time: 69.1 us; the launch traced here: 68.9 us
  Pallas kernels  59 us (85%)
  local copies, waits for them, and re-layouts  9.18 us (13%)
    pallas_call x1, Pallas kernels, local(): pl.pallas_call(body, out_shape=(jax.ShapeDtypeStruct(slabs, BF16), jax.Sh...  59 us
    unnamed x23, local copies, waits for them, and re-layouts  9.18 us

profile of v1, /device:TPU:1, one launch (start us, length us, event | category | flops | bytes accessed | tf_op | source)
XLA Modules:
  0.0 68.9 jit_solution(13951363736864419408)
XLA Ops:
  0.6 0.0 copy-start.1
  0.6 1.7 %copy.18.table = f32[2,6,3312]{2,1,0:T(8,128)} copy(f32[2,6,3312]{2,0,1:T(2,128)} %param.16) | data formatting | bytes 317952 | tf_op args[6]
  2.3 0.0 copy-done.1
  2.3 0.0 copy-start.2
  2.3 0.8 %copy.16 = bf16[2,2,12,12,192]{4,3,2,1,0:T(8,128)(2,1)} copy(bf16[2,2,12,12,192]{4,1,3,2,0:T(2,128)(2,1)S(1)} %copy-done.1) | data formatting | bytes 442368 | tf_op args[0]
  3.1 0.2 copy-done.2
  3.3 0.8 %copy.17 = bf16[2,2,12,12,192]{4,3,2,1,0:T(8,128)(2,1)} copy(bf16[2,2,12,12,192]{4,1,3,2,0:T(2,128)(2,1)S(1)} %copy-done.2) | data formatting | bytes 442368 | tf_op args[1]
  4.1 59.0 %shard_map.145 = (bf16[48,12,192]{2,1,0:T(8,128)(2,1)}, f32[192,576]{1,0:T(8,128)}, f32[192,192]{1,0:T(8,128)}, f32[1,192]{1,0:T(1,128)}, f32[1,192]{1,0:T(1,128)}, /*index=5*/f32[2,6,207]{2,1,0:T(8,128)}) custom-call(bf16[48,12,192]{2,1,0:T(8,128)(2,1)} %bitcast.8, bf16[48,12,192]{2,1,0:T(8,128)(2,1)} %bitcast.9, bf16[192,576]{1,0:T(8,128)(2,1)} %wqkv.1, ...), custom_call_target="tpu_custom_call" | custom-call | tf_op jit(solution)/shard_map/pallas_call | solution.py:507
  63.1 0.0 copy-start
  63.1 0.0 copy-start.4
  63.2 2.1 %copy.19 = bf16[2,2,12,12,192]{4,1,3,2,0:T(2,128)(2,1)} copy(bf16[2,2,12,12,192]{4,3,2,1,0:T(8,128)(2,1)} %bitcast.10) | data formatting | bytes 442368
  65.2 0.0 copy-done.4
  65.2 0.6 copy.20
  65.8 0.0 copy-done
  65.8 0.0 copy-start.3
  65.8 0.8 %copy.25 = f32[192,576]{1,0:T(8,128)} copy(f32[192,576]{1,0:T(8,128)S(1)} %copy-done) | data formatting | bytes 884736
  66.6 0.3 copy-done.3
  67.0 0.0 copy-start.6
  67.0 0.7 copy.26
  67.6 0.0 copy-done.6
  67.6 0.0 copy-start.5
  67.6 0.6 copy.27
  68.2 0.1 copy-done.5
  68.3 0.6 copy.28
Async XLA Ops:
  0.6 1.7 %copy-start.1 = (bf16[2,2,12,12,192]{4,1,3,2,0:T(2,128)(2,1)S(1)}, bf16[2,2,12,12,192]{4,1,3,2,0:T(2,128)(2,1)}, u32[]{:S(2)}) copy-start(bf16[2,2,12,12,192]{4,1,3,2,0:T(2,128)(2,1)} %param.10) | copy-start | bytes 663556
  2.3 1.0 %copy-start.2 = (bf16[2,2,12,12,192]{4,1,3,2,0:T(2,128)(2,1)S(1)}, bf16[2,2,12,12,192]{4,1,3,2,0:T(2,128)(2,1)}, u32[]{:S(2)}) copy-start(bf16[2,2,12,12,192]{4,1,3,2,0:T(2,128)(2,1)} %param.11) | copy-start | bytes 663556
  63.1 2.7 %copy-start = (f32[192,576]{1,0:T(8,128)S(1)}, f32[192,576]{1,0:T(8,128)}, u32[]{:S(2)}) copy-start(f32[192,576]{1,0:T(8,128)} %get-tuple-element.31) | copy-start | bytes 1327108
  63.1 2.1 %copy-start.4 = (f32[2,6,207]{2,1,0:T(8,128)S(1)}, f32[2,6,207]{2,1,0:T(8,128)}, u32[]{:S(2)}) copy-start(f32[2,6,207]{2,1,0:T(8,128)} %get-tuple-element.23) | copy-start | bytes 29812
  65.8 1.1 %copy-start.3 = (f32[192,192]{1,0:T(8,128)S(1)}, f32[192,192]{1,0:T(8,128)}, u32[]{:S(2)}) copy-start(f32[192,192]{1,0:T(8,128)} %get-tuple-element.32) | copy-start | bytes 442372
  67.0 0.7 copy-start.6
  67.6 0.7 copy-start.5

commit v2 on v1

--- a/solution.py
+++ b/solution.py
@@ -54,7 +54,7 @@
                     lev = 1 - dz
                     row = hh if dh else 3 + hh
                     lon = ww if dw else 6 + ww
-                    of_natural[s] = ((m * LEVELS + lev) * ROWS + row) * LONGS + lon
+                    of_natural[s] = ((m * ROWS + row) * LONGS + lon) * LEVELS + lev
                     there = 9 + hh if dh else hh
                     t, h = there // WH, there % WH
                     w = 6 + ww if dw else ww
@@ -72,7 +72,7 @@
     for b in range(12):
         for t in range(TYPES):
             for h in range(HEADS):
-                th, slot = t * HEADS + h, t * 8 + h
+                th, slot = t * HEADS + h, h * TYPES + t
                 out[5, b * 16 + slot] = th * 16 + b
                 out[6, th * 16 + b] = b * 16 + slot
     for zj in range(WZ):
@@ -113,8 +113,8 @@
     def body(
         tok, cot, wqkv, wproj, gain, shift, table, reg, keep, idx,
         out_tok, out_qkv, out_proj, out_gain, out_shift, out_bias,
-        ztok, zcot, sbuf, rbuf, xt, xg, dx, sb2, rb2,
-        xk, bm, dacc, w3, wt, pw, pwt, pnt, qkvt, dqt, ot,
+        sbuf, rbuf, xt, xg, dx, sb2, rb2,
+        xk, bm, dacc, by_x, w3, wt, pwt, pnt, qkvt, dqt, ot,
         accq, accp, accs, payf, payb, pairb, rsrc, plb, zbuf, fbuf, bmsg, brcv,
         s_h, r_h, s_o, r_o, s_p, r_p, s_1, r_1, s_2, r_2, s_3, r_3, s_4, r_4, s_b, r_b,
     ):
@@ -170,16 +170,18 @@
             pick = lax.broadcasted_iota(jnp.int32, (height, width), 0) == idx[row : row + 1, 0:width]
             return jnp.where(pick, 1.0, 0.0).astype(BF16)
 
-        for k in range(TOKENS // 24):
-            for half in range(2):
-                slab = 2 * k + half
-                at = 24 * k + 12 * half
-                ztok[at : at + 12, :] = tok[slab].astype(F32)
-                kept = keep[0, slab % ROWS].astype(F32)
-                zcot[at : at + 12, :] = cot[slab].astype(F32) * kept
+        own = cot[...].reshape(TOKENS, C).astype(F32)
+        line = LONGS * LEVELS
+        kept = jnp.concatenate(
+            [
+                own[k * line : (k + 1) * line] * keep[0, k % ROWS].astype(F32)
+                for k in range(MEMBERS * ROWS)
+            ],
+            axis=0,
+        )
         gather = onehot(2, PIECES, TOKENS)
-        piece_tok = dot(gather, ztok[...].astype(BF16))
-        piece_cot = dot(gather, zcot[...].astype(BF16))
+        piece_tok = dot(gather, tok[...].reshape(TOKENS, C))
+        piece_cot = dot(gather, kept.astype(BF16))
         sbuf[...] = jnp.concatenate([piece_tok, piece_cot], axis=1).astype(BF16)
 
         pl.semaphore_wait(barrier, len(partners))
@@ -191,7 +193,6 @@
             halo.append(copy)
         rbuf[0:112, :] = sbuf[0:112, :]
 
-        dacc[...] = jnp.zeros_like(dacc)
         accq[...] = jnp.zeros_like(accq)
         accp[...] = jnp.zeros_like(accp)
         accs[...] = jnp.zeros_like(accs)
@@ -201,10 +202,9 @@
                 for hi in range(WH):
                     kappa = (zi * WZ + zj) * WH + hi
                     b = zi * WH + hi
-                    for t in range(TYPES):
-                        xk[b * 16 + t * 8 : b * 16 + t * 8 + 6, zj * 256 : zj * 256 + FOLD] = table[
-                            t, :, kappa * FOLD : (kappa + 1) * FOLD
-                        ]
+                    xk[b * 16 : b * 16 + 12, zj * 256 : zj * 256 + FOLD] = table[
+                        :, :, kappa * FOLD : (kappa + 1) * FOLD
+                    ].reshape(TYPES * HEADS, FOLD)
         to_th = onehot(5, 192, 192)
         to_lane = onehot(4, 512, 384)
         rest = xk[...]
@@ -231,7 +231,11 @@
         for x in range(WW):
             moved = pltpu.roll(wide, (384 - 12 * (WW - 1 - x)) % 384, 1) if x < WW - 1 else wide
             for th in range(TYPES * HEADS):
-                bm[th, 12 * x : 12 * x + 12, :] = moved[16 * th : 16 * th + 12, 0:WIN]
+                dacc[th, 12 * x : 12 * x + 12, :] = moved[16 * th : 16 * th + 12, 0:WIN]
+        for th in range(TYPES * HEADS):
+            bm[th] = dacc[th].T
+        dacc[...] = jnp.zeros_like(dacc)
+        dx[...] = jnp.zeros_like(dx)
         for part in range(3):
             w3[part] = wqkv[:, part * C : (part + 1) * C]
         wt[...] = wqkv[...].astype(F32).T.astype(BF16)
@@ -251,13 +255,18 @@
             1.0, 0.0,
         ).astype(BF16)
 
+        ones = jnp.ones((C, C), BF16)
+
+        def mean(rows):
+            return dot(rows.astype(BF16), ones) * (1.0 / C)
+
         def window(w, carry):
             r0 = pl.multiple_of(w * WIN, 16)
             t = lax.div(w, MEMBERS)
             x = xt[pl.ds(r0, WIN), :]
             g = xg[pl.ds(r0, WIN), :]
-            centred = x - jnp.mean(x, axis=1, keepdims=True)
-            inv_std = lax.rsqrt(jnp.mean(centred * centred, axis=1, keepdims=True) + EPS)
+            centred = x - mean(x)
+            inv_std = lax.rsqrt(mean(centred * centred) + EPS)
             x_hat = centred * inv_std
             normed = (x_hat * gain[...] + shift[...]).astype(BF16)
             q = dot(normed, w3[0]).astype(BF16)
@@ -266,36 +275,32 @@
             d_att = dot_nt(g, wproj[...]).astype(BF16)
             qkvt[0 : 3 * C, :] = dot_nt(wt[...], normed).astype(BF16)
             qkvt[3 * C : 4 * C, :] = dot_nt(wproj[...], g).astype(BF16)
+            zero = jnp.zeros_like(k)
             for h in range(HEADS):
                 th = t * HEADS + h
                 mine = head_of == h
-                zero = jnp.zeros_like(q)
-                s = dot_nt(jnp.where(mine, q, zero), k) * score_scale + bm[th]
-                e = jnp.exp(s - jnp.max(s, axis=1, keepdims=True))
-                p = e * (1.0 / jnp.sum(e, axis=1, keepdims=True))
+                s = dot_nt(jnp.where(mine, k, zero), q) * score_scale + bm[th]
+                e = jnp.exp(s - jnp.max(s, axis=0, keepdims=True))
+                p = e * (1.0 / jnp.sum(e, axis=0, keepdims=True))
                 pb = p.astype(BF16)
-                d_p = dot_nt(jnp.where(mine, d_att, zero), v)
+                d_p = dot_nt(jnp.where(mine, v, zero), d_att)
                 lo = h * DH
-                ot[lo : lo + DH, :] = dot_nt(qkvt[2 * C + lo : 2 * C + lo + DH, :], pb).astype(BF16)
-                dqt[2 * C + lo : 2 * C + lo + DH, :] = dot(
-                    qkvt[3 * C + lo : 3 * C + lo + DH, :], pb
-                ).astype(BF16)
-                ds = p * (d_p - jnp.sum(p * d_p, axis=1, keepdims=True))
-                at = pl.multiple_of(th * 16, 16)
-                for xx in range(WW):
-                    dacc[xx, pl.ds(at, 12), :] += ds[12 * xx : 12 * xx + 12, :]
+                q_h, k_h, v_h, a_h = (qkvt[part * C + lo : part * C + lo + DH, :] for part in range(4))
+                ot[lo : lo + DH, :] = dot(v_h, pb).astype(BF16)
+                dqt[2 * C + lo : 2 * C + lo + DH, :] = dot_nt(a_h, pb).astype(BF16)
+                ds = p * (d_p - jnp.sum(p * d_p, axis=0, keepdims=True))
+                dacc[th] += ds
                 sc = (ds * score_scale).astype(BF16)
-                dqt[lo : lo + DH, :] = dot_nt(qkvt[C + lo : C + lo + DH, :], sc).astype(BF16)
-                dqt[C + lo : C + lo + DH, :] = dot(qkvt[lo : lo + DH, :], sc).astype(BF16)
+                dqt[lo : lo + DH, :] = dot(k_h, sc).astype(BF16)
+                dqt[C + lo : C + lo + DH, :] = dot_nt(q_h, sc).astype(BF16)
             accp[...] += dot(ot[...], g)
             accq[...] += dot_nt(dot_nt(eye, normed).astype(BF16), dqt[...])
             d_normed = dot_tn(dqt[...], wt[...])
             accs[0:1, :] += jnp.sum(d_normed * x_hat, axis=0, keepdims=True)
             accs[1:2, :] += jnp.sum(d_normed, axis=0, keepdims=True)
             d_hat = d_normed * gain[...]
-            m1 = jnp.mean(d_hat, axis=1, keepdims=True)
-            m2 = jnp.mean(d_hat * x_hat, axis=1, keepdims=True)
-            dx[pl.ds(r0, WIN), :] = (inv_std * (d_hat - m1 - x_hat * m2)).astype(BF16)
+            d_x = inv_std * (d_hat - mean(d_hat) - x_hat * mean(d_hat * x_hat))
+            dx[pl.ds(r0, WIN), 0:C] = d_x.astype(BF16)
             return carry
 
         lax.fori_loop(0, TYPES * MEMBERS, window, 0)
@@ -333,9 +338,14 @@
             p, copy = plane_copy(k)
             pl.when(p < BLOCKS)(copy.start)
 
+        by_x[...] = jnp.zeros_like(by_x)
         folded = jnp.zeros((192, 384), F32)
+        for th in range(TYPES * HEADS):
+            turned = dacc[th].T
+            for x in range(WW):
+                by_x[x, 16 * th : 16 * th + 12, :] = turned[12 * x : 12 * x + 12, :]
         for x in range(WW):
-            padded = jnp.concatenate([dacc[x], jnp.zeros((192, 384 - WIN), F32)], axis=1)
+            padded = jnp.concatenate([by_x[x], jnp.zeros((192, 384 - WIN), F32)], axis=1)
             off = 12 * (WW - 1 - x)
             folded = folded + (pltpu.roll(padded, off, 1) if off else padded)
         by_b = dot(onehot(6, 192, 192), folded.astype(BF16)).astype(BF16)
@@ -373,12 +383,8 @@
 
         for copy in back:
             copy.wait_recv()
-        ztok[...] = dot(pnt[...], rb2[...])
-        for k in range(TOKENS // 24):
-            for half in range(2):
-                slab = 2 * k + half
-                at = 24 * k + 12 * half
-                out_tok[slab] = (cot[slab].astype(F32) + ztok[at : at + 12, :]).astype(BF16)
+        returned = dot(pnt[...], rb2[...])[:, 0:C]
+        out_tok[...] = (own + returned).reshape(TOKENS // 2, 2, C).astype(BF16)
 
         def gather_copy(k):
             p = lax.rem(me_p + k, plane_n)
@@ -405,8 +411,7 @@
         for k in range(1, lon_n):
             bias[k - 1].wait_recv()
             sums = sums + brcv[k].astype(F32)
-        for t in range(TYPES):
-            out_bias[t] = sums[8 * t : 8 * t + 6, 0 : FOLD * 3 // 2]
+        out_bias[...] = sums[0 : TYPES * HEADS, 0 : FOLD * 3 // 2].reshape(HEADS, TYPES, FOLD * 3 // 2)
 
         for k in range(1, plane_n):
             p = lax.rem(me_p + plane_n - k, plane_n)
@@ -455,21 +460,19 @@
 
     sems = pltpu.SemaphoreType.DMA
     scratch = [
-        pltpu.VMEM((TOKENS, C), F32),
-        pltpu.VMEM((TOKENS, C), F32),
         pltpu.VMEM((PIECES, 2 * C), BF16),
         pltpu.VMEM((PIECES, 2 * C), BF16),
         pltpu.VMEM((TOKENS, C), F32),
         pltpu.VMEM((TOKENS, C), BF16),
-        pltpu.VMEM((TOKENS, C), BF16),
-        pltpu.VMEM((PIECES, C), BF16),
-        pltpu.VMEM((PIECES, C), BF16),
+        pltpu.VMEM((TOKENS, 256), BF16),
+        pltpu.VMEM((PIECES, 256), BF16),
+        pltpu.VMEM((PIECES, 256), BF16),
         pltpu.VMEM((192, 512), F32),
+        pltpu.VMEM((TYPES * HEADS, WIN, WIN), F32),
         pltpu.VMEM((TYPES * HEADS, WIN, WIN), F32),
         pltpu.VMEM((WW, 192, WIN), F32),
         pltpu.VMEM((3, C, C), BF16),
         pltpu.VMEM((3 * C, C), BF16),
-        pltpu.VMEM((16, 128), BF16),
         pltpu.VMEM((PIECES, TOKENS), BF16),
         pltpu.VMEM((TOKENS, PIECES), BF16),
         pltpu.VMEM((4 * C, WIN), BF16),
@@ -495,39 +498,51 @@
     return body, scratch
 
 
+def hand_over(*refs):
+    for source, target in zip(refs[:6], refs[6:]):
+        target[...] = source[...]
+
+
 def solution(mesh):
     lon_n, lev_n, lat_n = (mesh.shape[name] for name in ("lon", "lev", "lat"))
     body, scratch = make_body(lon_n, lev_n, lat_n)
     index = index_rows()
 
     def local(tokens, cotangent, w_qkv, w_proj, ln_gain, ln_shift, bias_table, region_ids, lat_keep):
-        slabs = (MEMBERS * LEVELS * ROWS, LONGS, C)
+        pairs = (TOKENS // LEVELS, LEVELS, C)
         vmem = pl.BlockSpec(memory_space=pltpu.VMEM)
         smem = pl.BlockSpec(memory_space=pltpu.SMEM)
-        back, g_qkv, g_proj, g_gain, g_shift, g_bias = pl.pallas_call(
+        shapes = (
+            jax.ShapeDtypeStruct(pairs, BF16),
+            jax.ShapeDtypeStruct((C, 3 * C), F32),
+            jax.ShapeDtypeStruct((C, C), F32),
+            jax.ShapeDtypeStruct((1, C), F32),
+            jax.ShapeDtypeStruct((1, C), F32),
+            jax.ShapeDtypeStruct((HEADS, TYPES, FOLD * 3 // 2), F32),
+        )
+        results = pl.pallas_call(
             body,
-            out_shape=(
-                jax.ShapeDtypeStruct(slabs, BF16),
-                jax.ShapeDtypeStruct((C, 3 * C), F32),
-                jax.ShapeDtypeStruct((C, C), F32),
-                jax.ShapeDtypeStruct((1, C), F32),
-                jax.ShapeDtypeStruct((1, C), F32),
-                jax.ShapeDtypeStruct((TYPES, HEADS, FOLD * 3 // 2), F32),
-            ),
+            out_shape=shapes,
             in_specs=[vmem] * 7 + [smem, smem, vmem],
             out_specs=(vmem,) * 6,
             scratch_shapes=scratch,
             compiler_params=pltpu.CompilerParams(
-                collective_id=0, has_side_effects=True, vmem_limit_bytes=56 * 1024 * 1024
+                collective_id=0, has_side_effects=True, vmem_limit_bytes=40 * 1024 * 1024
             ),
         )(
-            tokens.reshape(slabs), cotangent.reshape(slabs), w_qkv, w_proj,
-            ln_gain.reshape(1, C), ln_shift.reshape(1, C), bias_table,
-            region_ids, lat_keep.reshape(1, ROWS), jnp.asarray(index),
+            tokens.transpose(0, 2, 3, 1, 4).reshape(pairs),
+            cotangent.transpose(0, 2, 3, 1, 4).reshape(pairs),
+            w_qkv, w_proj, ln_gain.reshape(1, C), ln_shift.reshape(1, C),
+            bias_table.transpose(1, 0, 2), region_ids, lat_keep.reshape(1, ROWS), jnp.asarray(index),
         )
-        return (
-            back.reshape(tokens.shape), g_qkv, g_proj, g_gain.reshape(C), g_shift.reshape(C), g_bias,
-        )
+        back, g_qkv, g_proj, g_gain, g_shift, g_bias = pl.pallas_call(
+            hand_over,
+            out_shape=shapes,
+            in_specs=[vmem] * 6,
+            out_specs=(vmem,) * 6,
+        )(*results)
+        back = back.reshape(MEMBERS, ROWS, LONGS, LEVELS, C).transpose(0, 3, 1, 2, 4)
+        return back, g_qkv, g_proj, g_gain.reshape(C), g_shift.reshape(C), g_bias.transpose(1, 0, 2)
 
     return jax.shard_map(
         local,

time: 69.1 us -> 66.9 us (0.968)
  Pallas kernels: 59 us -> 56.4 us
    pallas_call x1 -> x2, Pallas kernels: 59 us -> 56.4 us  [the longest x1 54.2 us: local(): pl.pallas_call(body, out_shape=shapes, in_specs=[vmem] * 7 + [smem, smem,...]
    unnamed x23 -> x32, local copies, waits for them, and re-layouts: 9.18 us -> 9.48 us
where the time goes in v2:
time: 66.9 us; the launch traced here: 66.6 us
  Pallas kernels  56.4 us (84%)
  local copies, waits for them, and re-layouts  9.48 us (14%)
  between operations  0.7 us (1%)
    pallas_call x1, Pallas kernels, local(): pl.pallas_call(body, out_shape=shapes, in_specs=[vmem] * 7 + [smem, smem,...  54.2 us
    unnamed x32, local copies, waits for them, and re-layouts  9.48 us
    pallas_call x1, Pallas kernels, local(): pl.pallas_call(hand_over, out_shape=shapes, in_specs=[vmem] * 6, out_spec...  2.25 us

profile of v2, /device:TPU:1, one launch (start us, length us, event | category | flops | bytes accessed | tf_op | source)
XLA Modules:
  0.0 66.6 jit_solution(3971173318202718812)
XLA Ops:
  0.6 0.0 copy-start.11
  0.6 0.0 copy-start.12
  0.7 0.0 copy-start.10
  0.7 0.0 copy-start.15
  0.7 0.6 copy-done.11
  1.3 0.0 copy-done.12
  1.3 0.0 copy-done.10
  1.3 0.0 copy-done.15
  1.3 0.0 copy-start.1
  1.4 1.0 %copy-done.1 = bf16[2,2,12,12,192]{4,1,3,2,0:T(2,128)(2,1)S(1)} copy-done((bf16[2,2,12,12,192]{4,1,3,2,0:T(2,128)(2,1)S(1)}, bf16[2,2,12,12,192]{4,1,3,2,0:T(2,128)(2,1)}, u32[]{:S(2)}) %copy-start.1) | copy-done | bytes 221208
  2.3 0.0 copy-start.2
  2.3 1.0 %copy-done.2 = bf16[2,2,12,12,192]{4,1,3,2,0:T(2,128)(2,1)S(1)} copy-done((bf16[2,2,12,12,192]{4,1,3,2,0:T(2,128)(2,1)S(1)}, bf16[2,2,12,12,192]{4,1,3,2,0:T(2,128)(2,1)}, u32[]{:S(2)}) %copy-start.2) | copy-done | bytes 221208
  3.3 0.0 copy-start.4
  3.3 0.9 %copy-done.4 = bf16[192,576]{1,0:T(8,128)(2,1)S(1)} copy-done((bf16[192,576]{1,0:T(8,128)(2,1)S(1)}, bf16[192,576]{1,0:T(8,128)(2,1)}, u32[]{:S(2)}) %copy-start.4) | copy-done | bytes 221208
  4.2 0.0 copy-start.6
  4.2 0.9 %copy-done.6 = f32[2,6,3312]{2,0,1:T(2,128)S(1)} copy-done((f32[2,6,3312]{2,0,1:T(2,128)S(1)}, f32[2,6,3312]{2,0,1:T(2,128)}, u32[]{:S(2)}) %copy-start.6) | copy-done | bytes 159000
  5.1 0.0 copy-start.7
  5.1 0.9 %copy-done.7 = bf16[192,192]{1,0:T(8,128)(2,1)S(1)} copy-done((bf16[192,192]{1,0:T(8,128)(2,1)S(1)}, bf16[192,192]{1,0:T(8,128)(2,1)}, u32[]{:S(2)}) %copy-start.7) | copy-done | bytes 73752
  6.0 0.0 copy-start.8
  6.0 0.8 %copy-done.8 = s32[16,640]{1,0:T(8,128)S(1)} copy-done((s32[16,640]{1,0:T(8,128)S(1)}, s32[16,640]{1,0:T(8,128)}, u32[]{:S(2)}) %copy-start.8) | copy-done | bytes 40984
  6.8 54.2 %shard_map.145 = (bf16[288,2,192]{2,1,0:T(2,128)(2,1)S(1)}, f32[192,576]{1,0:T(8,128)S(1)}, f32[192,192]{1,0:T(8,128)S(1)}, f32[1,192]{1,0:T(1,128)S(1)}, f32[1,...) custom-call(bf16[288,2,192]{2,1,0:T(2,128)(2,1)S(1)} %bitcast.16, bf16[288,2,192]{2,1,0:T(2,128)(2,1)S(1)} %bitcast.17, ...), custom_call_target="tpu_custom_call" | custom-call | tf_op jit(solution)/shard_map/pallas_call | solution.py:523
  61.0 0.0 copy-start
  61.0 0.8 %copy-done = f32[192,576]{1,0:T(8,128)} copy-done((f32[192,576]{1,0:T(8,128)}, f32[192,576]{1,0:T(8,128)S(1)}, u32[]{:S(2)}) %copy-start) | copy-done | bytes 442392
  61.8 0.0 copy-start.3
  61.8 0.7 %copy-done.3 = bf16[288,2,192]{2,1,0:T(2,128)(2,1)} copy-done((bf16[288,2,192]{2,1,0:T(2,128)(2,1)}, bf16[288,2,192]{2,1,0:T(2,128)(2,1)S(1)}, u32[]{:S(2)}) %copy-start.3) | copy-done | bytes 221208
  62.5 0.0 copy-start.5
  62.5 0.7 %copy-done.5 = f32[192,192]{1,0:T(8,128)} copy-done((f32[192,192]{1,0:T(8,128)}, f32[192,192]{1,0:T(8,128)S(1)}, u32[]{:S(2)}) %copy-start.5) | copy-done | bytes 147480
  63.2 0.0 copy-start.9
  63.2 0.6 copy-done.9
  63.8 0.6 copy-done.13
  64.4 0.0 copy-done.14
  64.4 2.2 %shard_map.146 = (bf16[288,2,192]{2,1,0:T(2,128)(2,1)}, f32[192,576]{1,0:T(8,128)}, f32[192,192]{1,0:T(8,128)}, f32[1,192]{1,0:T(1,128)}, f32[1,192]{1,0:T(1,128)}, /*index=5*/f32[6,2,207]{2,1,0:T(2,128)}) custom-call(bf16[288,2,192]{2,1,0:T(2,128)(2,1)} %copy-done.3, f32[192,576]{1,0:T(8,128)} %copy-done, f32[192,192]{1,0:T(8,128)} %copy-done.5, ...), custom_call_target="tpu_custom_call" | custom-call | tf_op jit(solution)/shard_map/pallas_call | solution.py:538
  (2 shorter events, 0.0 us)
Async XLA Ops:
  0.6 0.7 %copy-start.11 = (f32[192]{0:T(256)S(1)}, f32[192]{0:T(256)}, u32[]{:S(2)}) copy-start(f32[192]{0:T(256)} %param.15) | copy-start | bytes 2308
  0.6 0.7 %copy-start.12 = (s32[2,12]{1,0:T(2,128)S(1)}, s32[2,12]{1,0:T(2,128)}, u32[]{:S(2)}) copy-start(s32[2,12]{1,0:T(2,128)} %reg.1) | copy-start | bytes 292
  0.7 0.7 %copy-start.10 = (f32[192]{0:T(256)S(1)}, f32[192]{0:T(256)}, u32[]{:S(2)}) copy-start(f32[192]{0:T(256)} %param.14) | copy-start | bytes 2308
  0.7 0.7 %copy-start.15 = (s32[12]{0:T(128)S(1)}, s32[12]{0:T(128)}, u32[]{:S(2)}) copy-start(s32[12]{0:T(128)} %param.18) | copy-start | bytes 148
  1.3 1.0 %copy-start.1 = (bf16[2,2,12,12,192]{4,1,3,2,0:T(2,128)(2,1)S(1)}, bf16[2,2,12,12,192]{4,1,3,2,0:T(2,128)(2,1)}, u32[]{:S(2)}) copy-start(bf16[2,2,12,12,192]{4,1,3,2,0:T(2,128)(2,1)} %param.10) | copy-start | bytes 663556
  2.3 1.0 %copy-start.2 = (bf16[2,2,12,12,192]{4,1,3,2,0:T(2,128)(2,1)S(1)}, bf16[2,2,12,12,192]{4,1,3,2,0:T(2,128)(2,1)}, u32[]{:S(2)}) copy-start(bf16[2,2,12,12,192]{4,1,3,2,0:T(2,128)(2,1)} %param.11) | copy-start | bytes 663556
  3.3 0.9 %copy-start.4 = (bf16[192,576]{1,0:T(8,128)(2,1)S(1)}, bf16[192,576]{1,0:T(8,128)(2,1)}, u32[]{:S(2)}) copy-start(bf16[192,576]{1,0:T(8,128)(2,1)} %wqkv.1) | copy-start | bytes 663556
  4.2 0.9 %copy-start.6 = (f32[2,6,3312]{2,0,1:T(2,128)S(1)}, f32[2,6,3312]{2,0,1:T(2,128)}, u32[]{:S(2)}) copy-start(f32[2,6,3312]{2,0,1:T(2,128)} %param.16) | copy-start | bytes 476932
  5.1 0.9 %copy-start.7 = (bf16[192,192]{1,0:T(8,128)(2,1)S(1)}, bf16[192,192]{1,0:T(8,128)(2,1)}, u32[]{:S(2)}) copy-start(bf16[192,192]{1,0:T(8,128)(2,1)} %wproj.1) | copy-start | bytes 221188
  6.0 0.8 %copy-start.8 = (s32[16,640]{1,0:T(8,128)S(1)}, s32[16,640]{1,0:T(8,128)}, u32[]{:S(2)}) copy-start(s32[16,640]{1,0:T(8,128)} %constant.2.clone.idx) | copy-start | bytes 122884
  61.0 0.8 %copy-start = (f32[192,576]{1,0:T(8,128)}, f32[192,576]{1,0:T(8,128)S(1)}, u32[]{:S(2)}) copy-start(f32[192,576]{1,0:T(8,128)S(1)} %get-tuple-element.19.refs_1_) | copy-start | bytes 1327108
  61.8 0.7 %copy-start.3 = (bf16[288,2,192]{2,1,0:T(2,128)(2,1)}, bf16[288,2,192]{2,1,0:T(2,128)(2,1)S(1)}, u32[]{:S(2)}) copy-start(bf16[288,2,192]{2,1,0:T(2,128)(2,1)S(1)} %get-tuple-element.18.refs_0_) | copy-start | bytes 663556
  62.5 0.7 %copy-start.5 = (f32[192,192]{1,0:T(8,128)}, f32[192,192]{1,0:T(8,128)S(1)}, u32[]{:S(2)}) copy-start(f32[192,192]{1,0:T(8,128)S(1)} %get-tuple-element.20.refs_2_) | copy-start | bytes 442372
  63.2 0.6 copy-start.9
  63.8 0.6 copy-start.13
  63.8 0.6 copy-start.14

commit v3 on v2

v3 whole, which is shorter than its diff:
```python
import math

import jax
import jax.numpy as jnp
import numpy as np
from jax import lax
from jax.experimental import pallas as pl
from jax.experimental.pallas import tpu as pltpu
from jax.sharding import PartitionSpec as P

MESH = pl.DeviceIdType.MESH
F32 = jnp.float32
BF16 = jnp.bfloat16

HEADS = 6
WZ = 2
WH = 6
WW = 12
MEMBERS = 2
LEVELS = 2
ROWS = 12
LONGS = 12
C = 192
DH = C // HEADS
WIN = WZ * WH * WW
TYPES = 2
TOKENS = MEMBERS * LEVELS * ROWS * LONGS
SPAN = 2 * WW - 1
FOLD = WH * SPAN
PIECES = 704
MASKED = -1000000000.0
EPS = 1e-05

BAND_ROWS = (WH, 3, 3)
BAND_FROM = (3, 9, 0)
BAND_TO = (0, 6, 9)
PIECE = []
for band, padded in ((0, 80), (1, 48), (2, 48)):
    for steps in range(4):
        start = PIECE[-1][3] + PIECE[-1][4] if PIECE else 0
        PIECE.append((band, steps // 2, steps % 2, start, padded))
REMOTE = [q for q, piece in enumerate(PIECE) if piece[0] == 2 or piece[1] + piece[2] > 0]
OWN = [q for q in range(len(PIECE)) if q not in REMOTE]
TYPE_AT = (0, 320)
TYPE_ROWS = (320, 384)
HALF = TOKENS // TYPES
BLOCKS = 12
INPUTS = 10


def index_rows():
    out = np.full((24, PIECES), -1, np.int32)
    for band, dz, dw, start, _ in PIECE:
        rows = BAND_ROWS[band]
        for m in range(MEMBERS):
            for hh in range(rows):
                for ww in range(6):
                    s = start + (m * rows + hh) * 6 + ww
                    row = BAND_FROM[band] + hh
                    lon = ww if dw else 6 + ww
                    natural = ((m * ROWS + row) * LONGS + lon) * LEVELS + 1 - dz
                    t, h = divmod(BAND_TO[band] + hh, WH)
                    w = 6 + ww if dw else ww
                    i = m * WIN + w * 12 + dz * WH + h
                    out[0, s] = natural
                    out[2, natural] = s
                    out[16 + t, s - TYPE_AT[t]] = i
                    out[18 + t, i] = s - TYPE_AT[t]
    for rr in range(SPAN):
        for zj in range(WZ):
            for hj in range(WH):
                out[4, (rr * WZ + zj) * WH + hj] = zj * 256 + hj * SPAN + SPAN - 1 - rr
    for b in range(12):
        for t in range(TYPES):
            for h in range(HEADS):
                th, slot = t * HEADS + h, h * TYPES + t
                out[5, b * 16 + slot] = th * 16 + b
                out[6, th * 16 + b] = b * 16 + slot
    for zj in range(WZ):
        for hj in range(WH):
            for r in range(SPAN):
                src = ((SPAN - 1 - r) * WZ + zj) * WH + hj
                flat = hj * SPAN + r
                out[7 + zj, flat] = src
                if hj < 3:
                    out[9 + zj, FOLD + flat] = src
                else:
                    out[11 + zj, flat - FOLD // 2] = src
                out[13 + zj, FOLD // 2 + flat] = src
    out[15, :384] = np.arange(384) % 12
    return out


def dot(a, b):
    return lax.dot_general(a, b, (((1,), (0,)), ((), ())), preferred_element_type=F32)


def dot_nt(a, b):
    return lax.dot_general(a, b, (((1,), (1,)), ((), ())), preferred_element_type=F32)


def dot_tn(a, b):
    return lax.dot_general(a, b, (((0,), (0,)), ((), ())), preferred_element_type=F32)


def make_body(lon_n, lev_n, lat_n):
    z_n = lon_n // 2
    y_n = lat_n // 2
    plane_n = 2 * y_n * lev_n
    PLANE = sorted(
        [(dh, dy, dx) for dh in range(2) for dy in range(y_n) for dx in range(lev_n)],
        key=lambda step: -((2, 1)[step[1]] * step[0] + (1 - step[0]) * step[1] + min(step[2], lev_n - step[2])),
    )
    Z_STEPS = sorted(range(1, z_n), key=lambda k: -min(k, z_n - k))
    LON_STEPS = sorted(range(1, lon_n), key=lambda k: -min(k % z_n, z_n - k % z_n))
    PEERS = range(plane_n - 1)
    total = MEMBERS * LEVELS * ROWS * LONGS * lon_n * lev_n * lat_n
    grad_scale = 1.0 / math.sqrt(total)
    score_scale = DH ** (-0.5)

    def body(*refs):
        inputs, held = refs[:INPUTS], refs[INPUTS + 6 : 2 * INPUTS + 6]
        run(inputs, *held, *refs[INPUTS : INPUTS + 6], *refs[2 * INPUTS + 6 :])

    def run(
        inputs, tok, cot, wqkv, wproj, gain, shift, table, reg, keep, idx,
        out_tok, out_qkv, out_proj, out_gain, out_shift, out_bias,
        pick, sbuf, rbuf, xt, xg, dx, sb2, rb2,
        xk, bm, dacc, by_x, w3, wt, to_win, to_piece, pnt,
        payb, pairb, rsrc, plb, zbuf, fbuf, bmsg, brcv,
        s_h, r_h, s_o, r_o, s_p, r_p, s_1, r_1, s_2, r_2, s_3, r_3, s_4, r_4, s_b, r_b, s_i,
        gsv, gpl, gz, s_gp, r_gp, s_g1, r_g1, s_g2, r_g2,
    ):
        o = lax.axis_index("lon")
        lv = lax.axis_index("lev")
        la = lax.axis_index("lat")
        core = lax.rem(la, 2)
        ylo = lax.div(la, 2)
        zz = lax.rem(o, z_n)
        yhi = lax.div(o, z_n)
        me_p = (yhi * y_n + ylo) * lev_n + lv

        def halo_dev(dz, dh, dw, sign):
            return {
                "lon": lax.rem(o + sign * dw + lon_n, lon_n),
                "lev": lax.rem(lv + sign * dz + lev_n, lev_n),
                "lat": lax.rem(la + sign * dh + lat_n, lat_n),
            }

        def plane_dev(p):
            ph = lax.div(p, y_n * lev_n)
            rest = lax.rem(p, y_n * lev_n)
            return {
                "lon": ph * z_n + zz,
                "lev": lax.rem(rest, lev_n),
                "lat": lax.div(rest, lev_n) * 2 + core,
            }

        def plane_peer(k, sign):
            dh, dy, dx = PLANE[k]
            there = lax.rem(yhi + dh, 2) * y_n + lax.rem(ylo + dy, y_n)
            return there * lev_n + lax.rem(lv + sign * dx + lev_n, lev_n)

        def z_dev(k):
            return {"lon": yhi * z_n + lax.rem(zz + k, z_n), "lev": lv, "lat": la}

        def lon_dev(k):
            return {"lon": lax.rem(o + k, lon_n), "lev": lv, "lat": la}

        pair_dev = {"lon": o, "lev": lv, "lat": ylo * 2 + 1 - core}

        def remote(src, dst, ssem, rsem, dev):
            return pltpu.make_async_remote_copy(
                src_ref=src, dst_ref=dst, send_sem=ssem, recv_sem=rsem,
                device_id=dev, device_id_type=MESH,
            )

        def halo_copy(q, source, target, ssem, rsem, sign):
            band, dz, dw, start, rows = PIECE[q]
            part = pl.ds(start, rows)
            dev = halo_dev(dz, 1 if band == 2 else 0, dw, sign)
            return remote(source.at[part], target.at[part], ssem.at[q], rsem.at[q], dev)

        held = (tok, cot, wqkv, wproj, gain, shift, table, reg, keep, idx)
        loads = [
            pltpu.make_async_copy(source, target, s_i.at[k])
            for k, (source, target) in enumerate(zip(inputs, held))
        ]
        for k in (9, 0, 1, 8):
            loads[k].start()
        partners = [
            halo_dev(q // 4, q // 2 % 2, q % 2, sign) for q in range(1, 8) for sign in (-1, 1)
        ]
        partners += [lon_dev(k) for k in LON_STEPS]
        partners += [plane_dev(plane_peer(k, 1)) for k in PEERS]
        partners.append(pair_dev)
        barrier = pltpu.get_barrier_semaphore()
        for dev in partners:
            pl.semaphore_signal(barrier, inc=1, device_id=dev, device_id_type=MESH)
        for k in (6, 7, 2, 3, 4, 5):
            loads[k].start()

        def onehot(row, height, width):
            pick = lax.broadcasted_iota(jnp.int32, (height, width), 0) == idx[row : row + 1, 0:width]
            return jnp.where(pick, 1.0, 0.0).astype(BF16)

        loads[9].wait()
        pick[...] = onehot(2, PIECES, TOKENS)
        for k in (0, 1, 8):
            loads[k].wait()
        own = cot[...].reshape(TOKENS, C).astype(F32)
        line = LONGS * LEVELS
        kept = jnp.concatenate(
            [
                own[k * line : (k + 1) * line] * keep[0, k % ROWS].astype(F32)
                for k in range(MEMBERS * ROWS)
            ],
            axis=0,
        ).astype(BF16)
        piece_tok = dot(pick[...], tok[...].reshape(TOKENS, C))
        piece_cot = dot(pick[...], kept)
        sbuf[...] = jnp.concatenate([piece_tok, piece_cot], axis=1).astype(BF16)

        pl.semaphore_wait(barrier, len(partners))
        halo = {q: halo_copy(q, sbuf, rbuf, s_h, r_h, -1) for q in REMOTE}
        back = {q: halo_copy(q, sb2, rb2, s_o, r_o, 1) for q in REMOTE}
        for copy in halo.values():
            copy.start()
        for q in OWN:
            start, rows = PIECE[q][3:]
            rbuf[start : start + rows, :] = sbuf[start : start + rows, :]

        for k in (6, 7, 2, 3, 4, 5):
            loads[k].wait()
        xk[...] = jnp.zeros_like(xk)
        for zi in range(WZ):
            for zj in range(WZ):
                for hi in range(WH):
                    kappa = (zi * WZ + zj) * WH + hi
                    b = zi * WH + hi
                    xk[b * 16 : b * 16 + 12, zj * 256 : zj * 256 + FOLD] = table[
                        :, :, kappa * FOLD : (kappa + 1) * FOLD
                    ].reshape(TYPES * HEADS, FOLD)
        to_th = onehot(5, 192, 192)
        to_lane = onehot(4, 512, 384)
        rest = xk[...]
        wide = jnp.zeros((192, 384), F32)
        for _ in range(3):
            term = rest.astype(BF16)
            rest = rest - term.astype(F32)
            wide = wide + dot(dot(to_th, term).astype(BF16), to_lane)
        lane_a = idx[15:16, 0:384]
        row_b = lax.broadcasted_iota(jnp.int32, (16, 384), 0)
        masked = []
        for t in range(TYPES):
            reg_a = jnp.zeros((16, 384), jnp.int32)
            reg_b = jnp.zeros((16, 384), jnp.int32)
            for z in range(WZ):
                for h in range(WH):
                    ident = reg[z, t * WH + h]
                    reg_a = jnp.where(lane_a == z * WH + h, ident, reg_a)
                    reg_b = jnp.where(row_b == z * WH + h, ident, reg_b)
            for h in range(HEADS):
                th = t * HEADS + h
                masked.append(jnp.where(reg_a == reg_b, wide[th * 16 : th * 16 + 16], MASKED))
        wide = jnp.concatenate(masked, axis=0)
        for x in range(WW):
            moved = pltpu.roll(wide, (384 - 12 * (WW - 1 - x)) % 384, 1) if x < WW - 1 else wide
            for th in range(TYPES * HEADS):
                dacc[th, 12 * x : 12 * x + 12, :] = moved[16 * th : 16 * th + 12, 0:WIN]
        for th in range(TYPES * HEADS):
            bm[th] = dacc[th].T
        dacc[...] = jnp.zeros_like(dacc)
        dx[...] = jnp.zeros_like(dx)
        for part in range(3):
            w3[part] = wqkv[:, part * C : (part + 1) * C]
        wt[...] = wqkv[...].astype(F32).T.astype(BF16)
        for t in range(TYPES):
            part = slice(TYPE_AT[t], TYPE_AT[t] + TYPE_ROWS[t])
            to_win[:, part] = onehot(16 + t, HALF, TYPE_ROWS[t])
            to_piece[part, :] = onehot(18 + t, TYPE_ROWS[t], HALF)
        pnt[...] = onehot(0, TOKENS, PIECES)

        head_of = lax.broadcasted_iota(jnp.int32, (1, C), 1) // DH
        eye = jnp.where(
            lax.broadcasted_iota(jnp.int32, (C, C), 0) == lax.broadcasted_iota(jnp.int32, (C, C), 1),
            1.0, 0.0,
        ).astype(BF16)

        ones = jnp.ones((C, C), BF16)

        def mean(rows):
            return dot(rows.astype(BF16), ones) * (1.0 / C)

        def stack(rows):
            zero = jnp.zeros_like(rows)
            return jnp.concatenate([jnp.where(head_of == h, rows, zero) for h in range(HEADS)], axis=0)

        def unstack(rows):
            out = rows[0:WIN]
            for h in range(1, HEADS):
                out = jnp.where(head_of == h, rows[h * WIN : (h + 1) * WIN], out)
            return out.astype(BF16)

        def window(w):
            r0 = w * WIN
            t = w // MEMBERS
            x = xt[r0 : r0 + WIN, :]
            g = xg[r0 : r0 + WIN, :]
            centred = x - mean(x)
            inv_std = lax.rsqrt(mean(centred * centred) + EPS)
            x_hat = centred * inv_std
            normed = (x_hat * gain[...] + shift[...]).astype(BF16)
            normed_t = dot_nt(eye, normed).astype(BF16)
            q = dot(normed, w3[0]).astype(BF16)
            k = dot(normed, w3[1]).astype(BF16)
            v = dot(normed, w3[2]).astype(BF16)
            d_att = dot_nt(g, wproj[...]).astype(BF16)
            k_heads, v_heads = stack(k), stack(v)
            s_all = dot_nt(k_heads, q)
            dp_all = dot_nt(v_heads, d_att)
            probs, scaled = [], []
            for h in range(HEADS):
                th = t * HEADS + h
                s = s_all[h * WIN : (h + 1) * WIN] * score_scale + bm[th]
                e = jnp.exp(s - jnp.max(s, axis=0, keepdims=True))
                p = e * (1.0 / jnp.sum(e, axis=0, keepdims=True))
                d_p = dp_all[h * WIN : (h + 1) * WIN]
                ds = p * (d_p - jnp.sum(p * d_p, axis=0, keepdims=True))
                if w % MEMBERS == 0:
                    dacc[th] = ds
                else:
                    dacc[th] += ds
                probs.append(p.astype(BF16))
                scaled.append((ds * score_scale).astype(BF16))
            probs = jnp.concatenate(probs, axis=0)
            scaled = jnp.concatenate(scaled, axis=0)
            att_t = dot_tn(v_heads, probs).astype(BF16)
            dq_t = dot_tn(k_heads, scaled).astype(BF16)
            d_v = unstack(dot(probs, d_att))
            d_k = unstack(dot(scaled, q))
            sums = (dot_nt(normed_t, dq_t), dot(normed_t, d_k), dot(normed_t, d_v), dot(att_t, g))
            return sums, (x_hat, inv_std, dq_t, d_k, d_v)

        def norm_back(w, x_hat, inv_std, dq_t, d_k, d_v):
            d_normed = dot_tn(dq_t, wt[0:C, :]) + dot_nt(d_k, w3[1]) + dot_nt(d_v, w3[2])
            d_hat = d_normed * gain[...]
            d_x = inv_std * (d_hat - mean(d_hat) - x_hat * mean(d_hat * x_hat))
            dx[w * WIN : (w + 1) * WIN, 0:C] = d_x.astype(BF16)
            return (
                jnp.sum(d_normed * x_hat, axis=0, keepdims=True),
                jnp.sum(d_normed, axis=0, keepdims=True),
            )

        def arrive(t):
            for q in REMOTE:
                if (PIECE[q][0] > 0) == (t > 0):
                    halo[q].wait_recv()
            part = slice(TYPE_AT[t], TYPE_AT[t] + TYPE_ROWS[t])
            arrived = dot(to_win[:, part], rbuf[part, :])
            xt[t * HALF : (t + 1) * HALF, :] = arrived[:, 0:C]
            xg[t * HALF : (t + 1) * HALF, :] = arrived[:, C : 2 * C].astype(BF16)

        def pack(t):
            part = slice(TYPE_AT[t], TYPE_AT[t] + TYPE_ROWS[t])
            sb2[part, :] = dot(to_piece[part, :], dx[t * HALF : (t + 1) * HALF, :]).astype(BF16)

        def depart(t):
            for q in REMOTE:
                if (PIECE[q][0] > 0) == (t > 0):
                    back[q].start()

        arrive(0)
        done = [window(m) for m in range(MEMBERS)]
        arrive(1)
        done += [window(MEMBERS + m) for m in range(MEMBERS)]
        sum_q, sum_k, sum_v, sum_p = (
            sum((one[0][part] for one in done[1:]), done[0][0][part]) for part in range(4)
        )

        halves = (jnp.concatenate([sum_q, sum_k], axis=1), jnp.concatenate([sum_v, sum_p], axis=1))
        payb[0] = halves[0].astype(BF16)
        payb[1] = halves[1].astype(BF16)
        pair = remote(payb.at[1 - core], pairb, s_p, r_p, pair_dev)
        pair.start()

        norms = [norm_back(w, *one[1]) for w, one in enumerate(done)]
        gsv[core] = jnp.zeros((8, 128), F32)
        for row in range(2):
            both = sum((one[row] for one in norms[1:]), norms[0][row])
            gsv[core, 2 * row : 2 * row + 1, :] = both[:, 0:128]
            gsv[core, 2 * row + 1 : 2 * row + 2, 0 : C - 128] = both[:, 128:C]
        gs_pair = remote(gsv.at[core], gsv.at[core], s_gp, r_gp, pair_dev)
        gs_pair_from = remote(gsv.at[1 - core], gsv.at[1 - core], s_gp, r_gp, pair_dev)
        gs_pair.start()

        pair.wait_recv()
        kept_half = payb[core].astype(F32)
        rsrc[...] = (kept_half + pairb[...].astype(F32)).astype(BF16)

        def block(ref, p):
            return ref.at[pl.ds(pl.multiple_of(p * 16, 16), 16)]

        def plane_copy(k):
            p = plane_peer(k, 1)
            return p, remote(
                block(rsrc, p), plb.at[k], s_1.at[k], r_1.at[k], plane_dev(p)
            )

        for k in PEERS:
            p, copy = plane_copy(k)
            pl.when(p < BLOCKS)(copy.start)
        pack(0)
        pack(1)
        for q in OWN:
            start, rows = PIECE[q][3:]
            rb2[start : start + rows, :] = sb2[start : start + rows, :]

        gs_pair_from.wait_recv()
        gpl[me_p] = gsv[0] + gsv[1]

        def gs_plane(k, p):
            return remote(gpl.at[p], gpl.at[p], s_g1.at[k], r_g1.at[k], plane_dev(plane_peer(k, 1)))

        def gs_z(k, z):
            return remote(gz.at[z], gz.at[z], s_g2.at[k], r_g2.at[k], z_dev(k))

        for k in PEERS:
            gs_plane(k, me_p).start()

        depart(0)
        depart(1)

        by_x[...] = jnp.zeros_like(by_x)
        folded = jnp.zeros((192, 384), F32)
        for th in range(TYPES * HEADS):
            turned = dacc[th].T
            for x in range(WW):
                by_x[x, 16 * th : 16 * th + 12, :] = turned[12 * x : 12 * x + 12, :]
        for x in range(WW):
            padded = jnp.concatenate([by_x[x], jnp.zeros((192, 384 - WIN), F32)], axis=1)
            off = 12 * (WW - 1 - x)
            folded = folded + (pltpu.roll(padded, off, 1) if off else padded)
        by_b = dot(onehot(6, 192, 192), folded.astype(BF16)).astype(BF16)
        for zj in range(WZ):
            pa, pb2, pc, pd = [dot(by_b, onehot(row + zj, 384, 256)) for row in (7, 9, 11, 13)]
            for zi in range(WZ):
                for u in range(2):
                    d = ((zi * WZ + zj) * 2 + u) * 2
                    b0 = (zi * WH + 3 * u) * 16
                    bmsg[d] = (pa[b0 : b0 + 16] + pb2[b0 + 16 : b0 + 32]).astype(BF16)
                    bmsg[d + 1] = (pc[b0 + 16 : b0 + 32] + pd[b0 + 32 : b0 + 48]).astype(BF16)
        def z_copy(k):
            return remote(zbuf.at[zz], zbuf.at[zz], s_2.at[k], r_2.at[k], z_dev(k))

        def z_from(k):
            z = lax.rem(zz + z_n - k, z_n)
            return remote(zbuf.at[z], zbuf.at[z], s_2.at[k], r_2.at[k], z_dev(k))

        @pl.when(me_p < BLOCKS)
        def _():
            part = rsrc[pl.ds(pl.multiple_of(me_p * 16, 16), 16), :].astype(F32)
            for k in PEERS:
                remote(block(rsrc, me_p), plb.at[k], s_1.at[k], r_1.at[k], pair_dev).wait_recv()
                part = part + plb[k].astype(F32)
            zbuf[zz] = part.astype(BF16)
            for k in Z_STEPS:
                z_copy(k).start()

        def gather_copy(k):
            p = plane_peer(k, 1)
            mine = block(fbuf.at[core], me_p)
            return remote(mine, mine, s_3.at[k], r_3.at[k], plane_dev(p))

        def pair_copy(k, p, side):
            there = block(fbuf.at[side], p)
            return remote(there, there, s_4.at[k], r_4.at[k], pair_dev)

        @pl.when(me_p < BLOCKS)
        def _():
            for k in range(1, z_n):
                z_from(k).wait_recv()
            part = zbuf[0].astype(F32)
            for k in range(1, z_n):
                part = part + zbuf[k].astype(F32)
            fbuf[core, pl.ds(pl.multiple_of(me_p * 16, 16), 16), :] = (part * grad_scale).astype(BF16)
            for k in PEERS:
                gather_copy(k).start()
            pair_copy(plane_n - 1, me_p, core).start()

        for k in PEERS:
            gs_plane(k, plane_peer(k, -1)).wait_recv()
        part = gpl[0]
        for p in range(1, plane_n):
            part = part + gpl[p]
        gz[zz] = part
        for k in Z_STEPS:
            gs_z(k, zz).start()

        bias = []
        for k in LON_STEPS:
            dev = lon_dev(k)
            copy = remote(bmsg.at[dev["lon"]], brcv.at[k], s_b.at[k], r_b.at[k], dev)
            copy.start()
            bias.append(copy)


        for copy in back.values():
            copy.wait_recv()
        returned = dot(pnt[...], rb2[...])[:, 0:C]
        out_tok[...] = (own + returned).reshape(TOKENS // 2, 2, C).astype(BF16)

        for k in reversed(PEERS):
            p = plane_peer(k, -1)

            @pl.when(p < BLOCKS)
            def _():
                here = block(fbuf.at[core], p)
                remote(here, here, s_3.at[k], r_3.at[k], pair_dev).wait_recv()
                pair_copy(k, p, core).start()

        for k in Z_STEPS:
            gs_z(k, lax.rem(zz + z_n - k, z_n)).wait_recv()
        part = gz[0]
        for z in range(1, z_n):
            part = part + gz[z]
        part = part * grad_scale
        for row, out in enumerate((out_gain, out_shift)):
            out[:, 0:128] = part[2 * row : 2 * row + 1, :]
            out[:, 128:C] = part[2 * row + 1 : 2 * row + 2, 0 : C - 128]

        for k in range(plane_n):
            p = plane_peer(k, -1)

            @pl.when(p < BLOCKS)
            def _():
                pair_copy(k, p, 1 - core).wait_recv()

        out_qkv[:, 0:384] = fbuf[0, 0:C, :].astype(F32)
        right = fbuf[1, 0:C, :].astype(F32)
        out_qkv[:, 384:576] = right[:, 0:C]
        out_proj[...] = right[:, C : 2 * C]

        sums = bmsg[o].astype(F32)
        for copy in bias:
            copy.wait_recv()
        for k in range(1, lon_n):
            sums = sums + brcv[k].astype(F32)
        out_bias[...] = sums[0 : TYPES * HEADS, 0 : FOLD * 3 // 2].reshape(HEADS, TYPES, FOLD * 3 // 2)


        for copy in [*halo.values(), *back.values(), *bias]:
            copy.wait_send()
        pair.wait_send()
        gs_pair.wait_send()
        for k in PEERS:
            gs_plane(k, me_p).wait_send()
        for k in Z_STEPS:
            gs_z(k, zz).wait_send()
        for k in PEERS:
            p, copy = plane_copy(k)
            pl.when(p < BLOCKS)(copy.wait_send)

        @pl.when(me_p < BLOCKS)
        def _():
            for k in Z_STEPS:
                z_copy(k).wait_send()
            for k in PEERS:
                gather_copy(k).wait_send()

        for k in range(plane_n):
            p = plane_peer(k, -1)

            @pl.when(p < BLOCKS)
            def _():
                pair_copy(k, p, core).wait_send()

    sems = pltpu.SemaphoreType.DMA
    scratch = [
        pltpu.VMEM((TOKENS // 2, 2, C), BF16),
        pltpu.VMEM((TOKENS // 2, 2, C), BF16),
        pltpu.VMEM((C, 3 * C), BF16),
        pltpu.VMEM((C, C), BF16),
        pltpu.VMEM((1, C), F32),
        pltpu.VMEM((1, C), F32),
        pltpu.VMEM((HEADS, TYPES, WZ * WZ * WH * FOLD), F32),
        pltpu.SMEM((LEVELS, ROWS), jnp.int32),
        pltpu.SMEM((1, ROWS), jnp.int32),
        pltpu.VMEM((24, PIECES), jnp.int32),
        pltpu.VMEM((PIECES, TOKENS), BF16),
        pltpu.VMEM((PIECES, 2 * C), BF16),
        pltpu.VMEM((PIECES, 2 * C), BF16),
        pltpu.VMEM((TOKENS, C), F32),
        pltpu.VMEM((TOKENS, C), BF16),
        pltpu.VMEM((TOKENS, 256), BF16),
        pltpu.VMEM((PIECES, 256), BF16),
        pltpu.VMEM((PIECES, 256), BF16),
        pltpu.VMEM((192, 512), F32),
        pltpu.VMEM((TYPES * HEADS, WIN, WIN), F32),
        pltpu.VMEM((TYPES * HEADS, WIN, WIN), F32),
        pltpu.VMEM((WW, 192, WIN), F32),
        pltpu.VMEM((3, C, C), BF16),
        pltpu.VMEM((3 * C, C), BF16),
        pltpu.VMEM((HALF, PIECES), BF16),
        pltpu.VMEM((PIECES, HALF), BF16),
        pltpu.VMEM((TOKENS, PIECES), BF16),
        pltpu.VMEM((2, 16 * BLOCKS, 384), BF16),
        pltpu.VMEM((16 * BLOCKS, 384), BF16),
        pltpu.VMEM((16 * BLOCKS, 384), BF16),
        pltpu.VMEM((plane_n, 16, 384), BF16),
        pltpu.VMEM((z_n, 16, 384), BF16),
        pltpu.VMEM((2, 16 * BLOCKS, 384), BF16),
        pltpu.VMEM((16, 16, 256), BF16),
        pltpu.VMEM((16, 16, 256), BF16),
        *[sems((len(PIECE),))] * 4, sems, sems,
        sems((plane_n,)), sems((plane_n,)), sems((z_n,)), sems((z_n,)),
        sems((plane_n,)), sems((plane_n,)), sems((plane_n,)), sems((plane_n,)),
        sems((lon_n,)), sems((lon_n,)), sems((INPUTS,)),
        pltpu.VMEM((2, 8, 128), F32),
        pltpu.VMEM((plane_n, 8, 128), F32),
        pltpu.VMEM((z_n, 8, 128), F32),
        sems, sems, sems((plane_n,)), sems((plane_n,)), sems((z_n,)), sems((z_n,)),
    ]
    return body, scratch


def hand_over(*refs):
    for source, target in zip(refs[:6], refs[6:]):
        target[...] = source[...]


def solution(mesh):
    lon_n, lev_n, lat_n = (mesh.shape[name] for name in ("lon", "lev", "lat"))
    body, scratch = make_body(lon_n, lev_n, lat_n)
    index = index_rows()

    def local(tokens, cotangent, w_qkv, w_proj, ln_gain, ln_shift, bias_table, region_ids, lat_keep):
        pairs = (TOKENS // LEVELS, LEVELS, C)
        vmem = pl.BlockSpec(memory_space=pltpu.VMEM)
        shapes = (
            jax.ShapeDtypeStruct(pairs, BF16),
            jax.ShapeDtypeStruct((C, 3 * C), F32),
            jax.ShapeDtypeStruct((C, C), F32),
            jax.ShapeDtypeStruct((1, C), F32),
            jax.ShapeDtypeStruct((1, C), F32),
            jax.ShapeDtypeStruct((HEADS, TYPES, FOLD * 3 // 2), F32),
        )
        results = pl.pallas_call(
            body,
            out_shape=tuple(pltpu.VMEM(s.shape, s.dtype) for s in shapes),
            in_specs=[pl.BlockSpec(memory_space=pl.ANY)] * INPUTS,
            out_specs=(vmem,) * 6,
            scratch_shapes=scratch,
            compiler_params=pltpu.CompilerParams(
                collective_id=0, has_side_effects=True, vmem_limit_bytes=60 * 1024 * 1024
            ),
        )(
            tokens.transpose(0, 2, 3, 1, 4).reshape(pairs),
            cotangent.transpose(0, 2, 3, 1, 4).reshape(pairs),
            w_qkv, w_proj, ln_gain.reshape(1, C), ln_shift.reshape(1, C),
            bias_table.transpose(1, 0, 2), region_ids, lat_keep.reshape(1, ROWS), jnp.asarray(index),
        )
        back, g_qkv, g_proj, g_gain, g_shift, g_bias = pl.pallas_call(
            hand_over,
            out_shape=shapes,
            in_specs=[vmem] * 6,
            out_specs=(vmem,) * 6,
            compiler_params=pltpu.CompilerParams(vmem_limit_bytes=8 * 1024 * 1024),
        )(*results)
        back = back.reshape(MEMBERS, ROWS, LONGS, LEVELS, C).transpose(0, 3, 1, 2, 4)
        return back, g_qkv, g_proj, g_gain.reshape(C), g_shift.reshape(C), g_bias.transpose(1, 0, 2)

    return jax.shard_map(
        local,
        mesh=mesh,
        in_specs=(
            P(None, "lev", "lat", "lon", None),
            P(None, "lev", "lat", "lon", None),
            P(), P(), P(), P(),
            P(("lev", "lat"), None, None),
            P("lev", "lat"),
            P("lat"),
        ),
        out_specs=(
            P(None, "lev", "lat", "lon", None),
            P(), P(), P(), P(),
            P(("lev", "lat"), None, "lon"),
        ),
        check_vma=False,
    )
```

time: 66.9 us -> 50.3 us (0.75)
  local copies, waits for them, and re-layouts: 9.48 us -> 0 us
  Pallas kernels: 56.4 us -> 49.6 us
    unnamed x32 -> x0, local copies, waits for them, and re-layouts: 9.48 us -> none
    pallas_call x1, Pallas kernels: 54.2 us -> 48.5 us  [local(): pl.pallas_call(body, out_shape=tuple((pltpu.VMEM(s.shape, s.dtype) for s...]
    pallas_call x1, Pallas kernels: 2.25 us -> 1.09 us  [local(): pl.pallas_call(hand_over, out_shape=shapes, in_specs=[vmem] * 6, out_spec...]
where the time goes in v3:
time: 50.3 us; the launch traced here: 50.2 us
  Pallas kernels  49.6 us (99%)
  between operations  0.64 us (1%)
    pallas_call x1, Pallas kernels, local(): pl.pallas_call(body, out_shape=tuple((pltpu.VMEM(s.shape, s.dtype) for s...  48.5 us
    pallas_call x1, Pallas kernels, local(): pl.pallas_call(hand_over, out_shape=shapes, in_specs=[vmem] * 6, out_spec...  1.09 us

profile of v3, /device:TPU:1, one launch (start us, length us, event | category | flops | bytes accessed | tf_op | source)
XLA Modules:
  0.0 50.2 jit_solution(5814223645067147909)
XLA Ops:
  0.6 48.5 %shard_map.145 = (bf16[288,2,192]{2,1,0:T(2,128)(2,1)S(1)}, f32[192,576]{1,0:T(8,128)S(1)}, f32[192,192]{1,0:T(8,128)S(1)}, f32[1,192]{1,0:T(1,128)S(1)}, f32[1,...) custom-call(bf16[288,2,192]{2,1,0:T(2,128)(2,1)} %bitcast.16, bf16[288,2,192]{2,1,0:T(2,128)(2,1)} %bitcast.17, ...), custom_call_target="tpu_custom_call" | custom-call | tf_op jit(solution)/shard_map/pallas_call | solution.py:648
  49.1 1.1 %shard_map.146 = (bf16[288,2,192]{2,1,0:T(2,128)(2,1)}, f32[192,576]{1,0:T(8,128)}, f32[192,192]{1,0:T(8,128)}, f32[1,192]{1,0:T(1,128)}, f32[1,192]{1,0:T(1,128)}, /*index=5*/f32[6,2,207]{2,1,0:T(2,128)}) custom-call(bf16[288,2,192]{2,1,0:T(2,128)(2,1)S(1)} %get-tuple-element.18.refs_0_, f32[192,576]{1,0:T(8,128)S(1)} %get-tuple-element.19.refs_1_, ...), custom_call_target="tpu_custom_call" | custom-call | tf_op jit(solution)/shard_map/pallas_call | solution.py:663
